TPU v7x, 256 devices: a whole 4x4x8 slice. The times are simulated.
256 devices in a mesh: dp: 4 (over x), tm: 4 (over y_lo, core), height: 16 (over y_hi, z).
Axes of the slice: x: 4, y: 4 (y_hi: 2, y_lo: 2; y = y_hi * 2 + y_lo), z: 8, core: 2. Of those that a mesh axis runs over, the one named last changes fastest.
Arguments:
- latent: bfloat16 [4, 8, 64, 16, 512], P('dp', 'tm', 'height'), may hold values from -6 to 6
- out_grad: bfloat16 [4, 8, 128, 32, 256], P('dp', 'tm', 'height'), may hold values from -6 to 6
- w_first: bfloat16 [27, 512, 512], P(None, None, 'height'), may hold values from -0.0546875 to 0.0546875
- w_second: bfloat16 [27, 512, 256], replicated, may hold values from -0.0546875 to 0.0546875
Outputs:
- grad_input: bfloat16 [4, 8, 64, 16, 512], P('dp', 'tm', 'height')
- grad_w2: float32 [512, 27, 256], P(('tm', 'height'))
All inputs are finite; a program needn't handle non-finite values.
Results may differ from a plain program's by a relative error of at most 0.017.
Values may be sent and summed in bfloat16 or wider, within the bound.
A program may use at most 128 MiB of HBM per device.

v0:
```python
import math

import jax
import jax.numpy as jnp
from jax import lax
from jax.sharding import PartitionSpec as P


def shifted(block, axis, distance):
    devices = range(lax.axis_size(axis))
    route = [(i - distance, i) for i in devices if i - distance in devices]
    return lax.ppermute(block, axis, route)


def with_halo(block, sides, width):
    for axis, dim in sides:
        count = lax.axis_size(axis)
        forward = [(i, i + 1) for i in range(count - 1)]
        backward = [(target, source) for source, target in forward]
        low = lax.ppermute(
            lax.slice_in_dim(block, block.shape[dim] - width, None, axis=dim), axis, forward
        )
        high = lax.ppermute(lax.slice_in_dim(block, 0, width, axis=dim), axis, backward)
        block = jnp.concatenate([low, block, high], axis=dim)
    return block


def convolve(padded, kernel, layout):
    result = lax.conv_general_dilated(
        padded[None],
        kernel,
        (1, 1, 1),
        "VALID",
        dimension_numbers=("NDHWC", layout, "NDHWC"),
        preferred_element_type=jnp.float32,
    )
    return result[0]


def silu_slope(values):
    sigmoid_v = jax.nn.sigmoid(values)
    return sigmoid_v * (1.0 + values * (1.0 - sigmoid_v))


def with_past(tensor):
    earlier = shifted(tensor[tensor.shape[0] - 2 :], "tm", 1)
    return jnp.concatenate([earlier, tensor], axis=0)


def with_future(tensor):
    following = shifted(tensor[:2], "tm", -1)
    return jnp.concatenate([tensor, following], axis=0)


def with_rims(tensor):
    banded = with_halo(tensor, (("height", 1),), 1)
    return jnp.pad(banded, ((0, 0), (0, 0), (1, 1), (0, 0)))


def on_device(latent, out_grad, w_first, w_second):
    inputs = latent[0]
    cot_block = out_grad[0]
    frames, row_count, col_count, in_width = inputs.shape
    kernel_one = lax.all_gather(w_first, "height", axis=2, tiled=True).reshape(
        3, 3, 3, in_width, in_width
    )
    pre_act = convolve(with_rims(with_past(inputs)), kernel_one, "DHWIO")
    act_out = jax.nn.silu(pre_act).astype(jnp.bfloat16)
    kernel_two = lax.rev(w_second.reshape(3, 3, 3, in_width, -1), (0, 1, 2))
    grad_up = convolve(with_rims(with_future(cot_block)), kernel_two, "DHWOI")
    grad_act = grad_up.reshape(frames, row_count, 2, col_count, 2, in_width).sum(axis=(2, 4))
    grad_pre = (grad_act * silu_slope(pre_act)).astype(jnp.bfloat16)
    grad_in = convolve(with_rims(with_future(grad_pre)), lax.rev(kernel_one, (0, 1, 2)), "DHWOI")
    grad_input = grad_in.astype(jnp.bfloat16)[None]
    act_ext = with_rims(with_past(act_out))
    upsampled = jnp.repeat(jnp.repeat(act_ext, 2, axis=1), 2, axis=2)[:, 1:-1, 1:-1]
    channel_block = lax.slice_in_dim(
        upsampled,
        0,
        in_width // lax.axis_size(("tm", "height")) * lax.axis_size(("tm", "height")),
        axis=3,
    )
    tap_terms = []
    for depth_tap in range(3):
        for row_tap in range(3):
            for col_tap in range(3):
                window = channel_block[
                    depth_tap : depth_tap + frames,
                    row_tap : row_tap + 2 * row_count,
                    col_tap : col_tap + 2 * col_count,
                ]
                tap_terms.append(
                    lax.dot_general(
                        window,
                        cot_block,
                        (((0, 1, 2), (0, 1, 2)), ((), ())),
                        preferred_element_type=jnp.float32,
                    )
                )
    shares = lax.psum_scatter(
        jnp.stack(tap_terms, axis=1), ("tm", "height"), scatter_dimension=0, tiled=True
    )
    cell_total = (
        lax.axis_size("dp")
        * frames
        * lax.axis_size("tm")
        * 4
        * row_count
        * lax.axis_size("height")
        * col_count
    )
    rescale = 1.0 / math.sqrt(float(cell_total))
    grad_w2 = lax.psum(shares.astype(jnp.bfloat16), "dp").astype(jnp.float32) * rescale
    return (grad_input, grad_w2)


def solution(mesh):
    placed = (
        P("dp", "tm", "height", None, None),
        P("dp", "tm", "height", None, None),
        P(None, None, "height"),
        P(),
    )
    return jax.shard_map(
        on_device,
        mesh=mesh,
        in_specs=placed,
        out_specs=(P("dp", "tm", "height", None, None), P(("tm", "height"), None, None)),
        check_vma=False,
    )
```

profile of v0, /device:TPU:8, one launch (start us, length us, event | category | flops | bytes accessed | tf_op | source)
XLA Modules:
  0.0 663.8 jit_solution(5082393633621263896)
XLA Ops:
  7.9 1.9 collective-permute-start
  9.9 2.4 collective-permute-start.3
  12.3 4.6 collective-permute-done.3
  19.0 4.5 collective-permute-start.4
  25.7 4.5 collective-permute-start.1
  32.9 1.4 fusion.52
  35.3 7.2 %convolution_select_fusion = f32[2,8,8,5,512]{4,2,3,1,0:T(8,128)S(1)} fusion(bf16[3,3,3,512,256]{4,3,2,1,0:T(8,128)(2,1)} %bitcast.337, bf16[4,10,1,7,2,256]{5,3,4,1,0,2:T(8,128)(2,1)S(1)} %slice.174, bf16[4,10,1,8,5,256]{5,3,4,1,0,2:T(8,128)(2,1)S(1)} %copy.9, pred[8,5]{0,1:T(8,128)(4,1)} %constant.34), kind=kOutput, calls=%fused_computation.12 | convolution fusion | flops 4533616640 | bytes 9494568 | tf_op jit(solution)/shard_map/conv_general_dilated | solution.py:29
  44.9 163.4 %all-gather.2.cloned.1.call-done = bf16[27,512,512]{1,2,0:T(8,128)(2,1)} async-done(((bf16[27,512,32]{1,2,0:T(8,128)(2,1)}), bf16[27,512,512]{1,2,0:T(8,128)(2,1)}) %all-gather.2.cloned.1.call-update) | async-done | bytes 14155792 | tf_op jit(solution)/shard_map/all_gather | solution.py:64
  208.4 7.9 %convolution_select_fusion.2 = f32[2,4,8,3,512]{4,2,3,1,0:T(8,128)S(1)} fusion(bf16[3,3,3,512,512]{3,4,2,1,0:T(8,128)(2,1)} %bitcast.335, bf16[4,6,1,7,2,512]{5,3,4,1,0,2:T(8,128)(2,1)S(1)} %slice.176, bf16[4,6,1,8,3,512]{5,3,4,1,0,2:T(8,128)(2,1)S(1)} %copy.13, pred[8,3]{0,1:T(4,128)(4,1)S(1)} %copy-done.1), kind=kOutput, calls=%fused_computation.68 | convolution fusion | flops 2720956416 | bytes 15482904 | tf_op jit(solution)/shard_map/conv_general_dilated | solution.py:29
  216.9 1.9 collective-permute-start.9
  218.8 4.4 collective-permute-done.9
  224.7 4.6 collective-permute-start.10
  230.2 1.5 collective-permute-done.10
  233.4 4.3 fusion.133
  237.8 12.0 %fusion.132 = (bf16[2,8,32,512]{3,0,2,1:T(2,128)(2,1)S(1)}, bf16[2,8,32,512]{3,0,2,1:T(2,128)(2,1)S(1)}, bf16[2,8,32,512]{3,0,2,1:T(2,128)(2,1)S(1)}, bf16[2,8,3...) fusion(bf16[4,12,36,512]{3,0,2,1:T(4,128)(2,1)S(1)} %bitcast.321), kind=kLoop, calls=%fused_computation.190 | loop fusion | bytes 19922944 | tf_op jit(solution)/shard_map/slice | solution.py:87
  281.1 1.9 collective-permute-start.6
  283.0 2.5 collective-permute-done.6
  287.0 5.2 collective-permute-start.7
  293.0 1.5 collective-permute-done.7
  295.7 8.0 %fusion.33 = bf16[2,4,8,3,512]{4,2,3,1,0:T(8,128)(2,1)S(1)} fusion(bf16[3,3,3,512,512]{3,4,2,1,0:T(8,128)(2,1)} %bitcast.336, bf16[4,6,1,7,2,512]{5,3,4,1,0,2:T(8,128)(2,1)S(1)} %slice.180, bf16[4,6,1,8,3,512]{5,3,4,1,0,2:T(8,128)(2,1)S(1)} %copy.18, pred[8,3]{0,1:T(4,128)(4,1)S(1)} %copy-done.1), kind=kOutput, calls=%fused_computation.71 | convolution fusion | flops 2721054720 | bytes 15286296 | tf_op jit(solution)/shard_map/conv_general_dilated | solution.py:29
  303.8 295.3 %reduce-scatter.2.cloned.1.call-done = f32[8,27,256]{2,0,1:T(8,128)} async-done(((f32[512,27,256]{2,0,1:T(8,128)}), f32[8,27,256]{2,0,1:T(8,128)}) %reduce-scatter.2.cloned.1.call-update) | async-done | bytes 221200 | tf_op jit(solution)/shard_map/reduce_scatter | solution.py:100
  599.1 1.6 convert_element_type.25
  601.5 54.1 %all-reduce.6.cloned.1.call-done = bf16[8,27,256]{2,0,1:T(8,128)(2,1)} async-done(((bf16[8,27,256]{2,0,1:T(8,128)(2,1)}), bf16[8,27,256]{2,0,1:T(8,128)(2,1)}) %all-reduce.6.cloned.1.call-update) | async-done | bytes 110608 | tf_op jit(solution)/shard_map/psum | solution.py:113
  655.6 1.6 convert_multiply_fusion
  (80 shorter events, 51.1 us)
Async XLA Ops:
  7.2 201.2 %all-gather.2.cloned.1.call-start = ((), (), s32[]{:S(2)}) async-start(), calls=%async_computation.1 | async-start | bytes 15040512 | tf_op jit(solution)/shard_map/all_gather | solution.py:64
  7.9 591.2 %reduce-scatter.2.cloned.1.call-start = ((), (), s32[]{:S(2)}) async-start(), calls=%async_computation.2 | async-start | bytes 14376960 | tf_op jit(solution)/shard_map/reduce_scatter | solution.py:100
  7.9 15.6 %collective-permute-start = (bf16[2,8,32,256]{3,2,1,0:T(8,128)(2,1)}, bf16[2,8,32,256]{3,2,1,0:T(8,128)(2,1)S(1)}, u32[]{:S(2)}, u32[]{:S(2)}) collective-permute-start(bf16[2,8,32,256]{3,2,1,0:T(8,128)(2,1)} %bitcast.328), channel_id=1, source_target_pairs={{16,0},{32,16},{48,32},{17,1},{33,17},{49,33},{18,2},{34,18},{50,3... | collective-permute-start | bytes 786440 | tf_op jit(solution)/shard_map/ppermute | solution.py:12
  9.9 7.1 %collective-permute-start.3 = (bf16[2,4,16,512]{3,2,1,0:T(8,128)(2,1)}, bf16[2,4,16,512]{3,2,1,0:T(8,128)(2,1)S(1)}, u32[]{:S(2)}, u32[]{:S(2)}) collective-permute-start(bf16[2,4,16,512]{3,2,1,0:T(8,128)(2,1)} %bitcast.332), channel_id=1, source_target_pairs={{0,16},{16,32},{32,48},{1,17},{17,33},{33,49},{2,18},{18,34},{34,5... | collective-permute-start | bytes 393224 | tf_op jit(solution)/shard_map/ppermute | solution.py:12
  17.7 12.5 %collective-permute-start.5 = (bf16[4,1,16,512]{3,2,1,0:T(8,128)(2,1)S(1)}, bf16[4,1,16,512]{3,2,1,0:T(8,128)(2,1)S(1)}, u32[]{:S(2)}, u32[]{:S(2)}) collective-permute-start(bf16[4,1,16,512]{3,2,1,0:T(8,128)(2,1)S(1)} %get-tuple-element.40), channel_id=1, source_target_pairs={{1,0},{2,1},{3,2},{4,3},{5,4},{6,5},{7,6},{8,7},{9,8},{10,9},{11,1... | collective-permute-start | bytes 196616 | tf_op jit(solution)/shard_map/ppermute | solution.py:23
  19.0 11.2 %collective-permute-start.4 = (bf16[4,1,16,512]{3,2,1,0:T(8,128)(2,1)S(1)}, bf16[4,1,16,512]{3,2,1,0:T(8,128)(2,1)S(1)}, u32[]{:S(2)}, u32[]{:S(2)}) collective-permute-start(bf16[4,1,16,512]{3,2,1,0:T(8,128)(2,1)S(1)} %get-tuple-element.39), channel_id=1, source_target_pairs={{0,1},{1,2},{2,3},{3,4},{4,5},{5,6},{6,7},{7,8},{8,9},{9,10},{10,1... | collective-permute-start | bytes 196616 | tf_op jit(solution)/shard_map/ppermute | solution.py:20
  24.4 7.8 %collective-permute-start.2 = (bf16[4,1,32,256]{3,2,1,0:T(8,128)(2,1)S(1)}, bf16[4,1,32,256]{3,2,1,0:T(8,128)(2,1)S(1)}, u32[]{:S(2)}, u32[]{:S(2)}) collective-permute-start(bf16[4,1,32,256]{3,2,1,0:T(8,128)(2,1)S(1)} %get-tuple-element.32), channel_id=1, source_target_pairs={{1,0},{2,1},{3,2},{4,3},{5,4},{6,5},{7,6},{8,7},{9,8},{10,9},{11,1... | collective-permute-start | bytes 196616 | tf_op jit(solution)/shard_map/ppermute | solution.py:23
  25.7 7.3 %collective-permute-start.1 = (bf16[4,1,32,256]{3,2,1,0:T(8,128)(2,1)S(1)}, bf16[4,1,32,256]{3,2,1,0:T(8,128)(2,1)S(1)}, u32[]{:S(2)}, u32[]{:S(2)}) collective-permute-start(bf16[4,1,32,256]{3,2,1,0:T(8,128)(2,1)S(1)} %get-tuple-element.31), channel_id=1, source_target_pairs={{0,1},{1,2},{2,3},{3,4},{4,5},{5,6},{6,7},{7,8},{8,9},{9,10},{10,1... | collective-permute-start | bytes 196616 | tf_op jit(solution)/shard_map/ppermute | solution.py:20
  35.3 173.1 %copy-start.1 = (pred[8,3]{0,1:T(4,128)(4,1)S(1)}, pred[8,3]{0,1:T(4,128)(4,1)}, u32[]{:S(2)}) copy-start(pred[8,3]{0,1:T(4,128)(4,1)} %constant.33) | copy-start | bytes 76
  216.9 6.3 collective-permute-start.9
  223.4 6.9 %collective-permute-start.11 = (bf16[4,1,16,512]{3,1,2,0:T(2,128)(2,1)S(1)}, bf16[4,1,16,512]{3,1,2,0:T(2,128)(2,1)S(1)}, u32[]{:S(2)}, u32[]{:S(2)}) collective-permute-start(bf16[4,1,16,512]{3,1,2,0:T(2,128)(2,1)S(1)} %get-tuple-element.36), channel_id=1, source_target_pairs={{1,0},{2,1},{3,2},{4,3},{5,4},{6,5},{7,6},{8,7},{9,8},{10,9},{11,1... | collective-permute-start | bytes 196616 | tf_op jit(solution)/shard_map/ppermute | solution.py:23
  224.7 7.1 %collective-permute-start.10 = (bf16[4,1,16,512]{3,1,2,0:T(2,128)(2,1)S(1)}, bf16[4,1,16,512]{3,1,2,0:T(2,128)(2,1)S(1)}, u32[]{:S(2)}, u32[]{:S(2)}) collective-permute-start(bf16[4,1,16,512]{3,1,2,0:T(2,128)(2,1)S(1)} %get-tuple-element.35), channel_id=1, source_target_pairs={{0,1},{1,2},{2,3},{3,4},{4,5},{5,6},{6,7},{7,8},{8,9},{9,10},{10,1... | collective-permute-start | bytes 196616 | tf_op jit(solution)/shard_map/ppermute | solution.py:20
  233.4 16.4 %copy-start = (bf16[1,2,8,32,256]{4,3,2,1,0:T(8,128)(2,1)S(1)}, bf16[1,2,8,32,256]{4,3,2,1,0:T(8,128)(2,1)}, u32[]{:S(2)}) copy-start(bf16[1,2,8,32,256]{4,3,2,1,0:T(8,128)(2,1)} %param.5) | copy-start | bytes 786436
  281.0 374.6 %all-reduce.6.cloned.1.call-start = ((), (), s32[]{:S(2)}) async-start(), calls=%async_computation.3 | async-start | bytes 221184 | tf_op jit(solution)/shard_map/psum | solution.py:113
  281.1 4.4 collective-permute-start.6
  285.7 7.3 %collective-permute-start.8 = (bf16[4,1,16,512]{3,1,2,0:T(2,128)(2,1)S(1)}, bf16[4,1,16,512]{3,1,2,0:T(2,128)(2,1)S(1)}, u32[]{:S(2)}, u32[]{:S(2)}) collective-permute-start(bf16[4,1,16,512]{3,1,2,0:T(2,128)(2,1)S(1)} %get-tuple-element.38), channel_id=1, source_target_pairs={{1,0},{2,1},{3,2},{4,3},{5,4},{6,5},{7,6},{8,7},{9,8},{10,9},{11,1... | collective-permute-start | bytes 196616 | tf_op jit(solution)/shard_map/ppermute | solution.py:23
  287.0 7.5 %collective-permute-start.7 = (bf16[4,1,16,512]{3,1,2,0:T(2,128)(2,1)S(1)}, bf16[4,1,16,512]{3,1,2,0:T(2,128)(2,1)S(1)}, u32[]{:S(2)}, u32[]{:S(2)}) collective-permute-start(bf16[4,1,16,512]{3,1,2,0:T(2,128)(2,1)S(1)} %get-tuple-element.37), channel_id=1, source_target_pairs={{0,1},{1,2},{2,3},{3,4},{4,5},{5,6},{6,7},{7,8},{8,9},{9,10},{10,1... | collective-permute-start | bytes 196616 | tf_op jit(solution)/shard_map/ppermute | solution.py:20
Sparse Core Ops, SparseCore 0:
  10.6 197.7 all-gather.1
  281.2 317.9 reduce-scatter.1
  602.0 53.5 all-reduce.5
where the time goes:
time: 664 us
  waiting for transfers between devices  531 us (80%)
  matrix products  54.3 us (8%)
  starting transfers between devices  32.3 us (5%)
  local copies, waits for them, and re-layouts  22.5 us (3%)
  between operations  14.1 us (2%)
  other arithmetic  9.86 us (1%)
    reduce_scatter x1, waiting for transfers between devices, on_device(): lax.psum_scatter(jnp.stack(tap_terms, axis=1), ('tm', 'height'), scatter_...  295 us
    all_gather x1, waiting for transfers between devices, on_device(): lax.all_gather(w_first, 'height', axis=2, tiled=True)  163 us
    psum x1, waiting for transfers between devices, on_device(): lax.psum(shares.astype(jnp.bfloat16), 'dp').astype(jnp.float32) * rescale  54.1 us
    dot_general x27, matrix products, on_device(): lax.dot_general(window, cot_block, (((0, 1, 2), (0, 1, 2)), ((), ())), pr...  31.2 us
    conv_general_dilated x3, matrix products, convolve(): lax.conv_general_dilated(padded[None], kernel, (1, 1, 1), 'VALID', dimens...  23.1 us
    ppermute x4, starting transfers between devices, with_halo(): lax.ppermute(lax.slice_in_dim(block, block.shape[dim] - width, None, axis...  18.9 us
    slice x2, local copies, waits for them, and re-layouts, on_device(): channel_block[depth_tap:depth_tap + frames, row_tap:row_tap + 2 * row_cou...  16.4 us
  transfers between devices with their start and end apart: 15, of which 11 were waited for; matrix products, arithmetic and copies ran while one was open for 4% of the time, Pallas kernels for 0%

commit v1 on v0

v1 whole, which is shorter than its diff:
```python
import functools
import math

import jax
import jax.numpy as jnp
import numpy as np
from jax import lax
from jax.experimental import pallas as pl
from jax.experimental.pallas import tpu as pltpu
from jax.sharding import PartitionSpec as P

MESH = pl.DeviceIdType.MESH
BF = jnp.bfloat16
F32 = jnp.float32
NZ = 8
NT = (((1,), (1,)), ((), ()))
NN = (((1,), (0,)), ((), ()))


def cell_sums():
    main = np.zeros((3, 3, 4, 16, 8, 32), np.float32)
    edge = np.zeros((2, 3, 16, 8, 32), np.float32)
    for b in range(3):
        for e in range(3):
            for c in range(16):
                cols = [2 * c + q + 1 - e for q in range(2) if 0 <= 2 * c + q + 1 - e < 32]
                for h in range(4):
                    for p in range(2):
                        row = 2 * h + p + 1 - b
                        if 0 <= row < 8:
                            main[b, e, h, c, row, cols] = 1.0
                if b == 0:
                    edge[0, e, c, 0, cols] = 1.0
                if b == 2:
                    edge[1, e, c, 7, cols] = 1.0
    return np.concatenate([main.reshape(576, 256), edge.reshape(96, 256)], axis=0)


def dot(a, b, dims):
    return lax.dot_general(a, b, dims, preferred_element_type=F32)


def body(
    scale,
    lat_in, og_in, wt_in, w2_in, sums_in, eye_in,
    gi_out, gw_out,
    xg, og, w, w2, g, gh, acc, q, qh, pre, ga, e1s, e1r, e2s, e2r,
    act, gp3, act3, act3t, hal3t, gi, pb, rp, ps, rr, gws, ra, sb, rb, fc, rc,
    ag_s, ag_r, wr_s, wr_r, wl_s, wl_r, w2_s, loc_s, e_s, e_r, pr_s, pr_r, rs_s, rs_r,
    a_s, a_r, b_s, b_r, c_s, c_r,
):
    x = lax.axis_index("dp")
    tm = lax.axis_index("tm")
    height = lax.axis_index("height")
    c = tm % 2
    ylo = tm // 2
    z = height % NZ
    yhi = height // NZ
    y = 2 * yhi + ylo

    def dev(x_, y_, z_, c_):
        return (x_, (y_ % 2) * 2 + c_, (y_ // 2) * NZ + z_)

    up_y, down_y = (y + 1) % 4, (y + 3) % 4
    up_z, down_z = (z + 1) % NZ, (z + NZ - 1) % NZ

    def remote(src, dst, ssem, rsem, target):
        return pltpu.make_async_remote_copy(
            src_ref=src, dst_ref=dst, send_sem=ssem, recv_sem=rsem,
            device_id=target, device_id_type=MESH,
        )

    y_own = 2 * (x // 2) + yhi
    z_own = 4 * (x % 2) + 2 * ylo
    x_src = 2 * (y // 2) + z // 4
    y_src = 2 * (y % 2) + (z % 4) // 2

    barrier = pltpu.get_barrier_semaphore()

    def greet(target):
        pl.semaphore_signal(barrier, inc=1, device_id=target, device_id_type=MESH)

    for d in range(1, 4):
        greet(dev(x, (y + d) % 4, z, c))
        greet(dev((x + d) % 4, y, z, c))
    greet(dev(x, y, z, 1 - c))
    for d in range(1, NZ):
        greet(dev(x, y, (z + d) % NZ, c))
    from_self = jnp.logical_and(x_src == x, y_src == y)
    for d in range(NZ):
        src_z = (z + d) % NZ
        if d == 0:
            @pl.when(jnp.logical_not(from_self))
            def _():
                greet(dev(x_src, y_src, z, c))
        else:
            greet(dev(x_src, y_src, src_z, c))
    pl.semaphore_wait(barrier, 22 - from_self.astype(jnp.int32))

    def slab(ref, y_, c_, f):
        return ref.at[2 * (2 * (y_ % 2) + c_) + f, y_ // 2]

    def block(ref, y_, c_):
        return ref.at[pl.ds(2 * (2 * (y_ % 2) + c_), 2), y_ // 2]

    arrays = ((og_in, og), (lat_in, xg))
    far = (y + 2) % 4

    def gather(n, i):
        src, ref = arrays[n]
        up, down, mate = dev(x, up_y, z, c), dev(x, down_y, z, c), dev(x, y, z, 1 - c)
        plan = {
            0: lambda: (src.at[0], slab(ref, y, c, 0), up),
            1: lambda: (src.at[1], slab(ref, y, c, 1), down),
            2: lambda: (src.at[1], slab(ref, y, c, 1), up),
            3: lambda: (src.at[0], slab(ref, y, c, 0), down),
            4: lambda: (src, block(ref, y, c), mate),
            5: lambda: (slab(ref, down_y, c, 0), slab(ref, down_y, c, 0), up),
            6: lambda: (slab(ref, up_y, c, 1), slab(ref, up_y, c, 1), down),
            7: lambda: (block(ref, down_y, c), block(ref, down_y, c), mate),
            8: lambda: (block(ref, up_y, c), block(ref, up_y, c), mate),
            9: lambda: (block(ref, far, c), block(ref, far, c), mate),
        }
        s, d, t = plan[i]()
        return remote(s, d, ag_s.at[n, i], ag_r.at[n, i], t)

    pos = (z + NZ - 4 * c) % NZ

    def right(k):
        s = (pos + NZ - k) % NZ
        slot = s % 4
        src = wt_in if k == 0 else w.at[:, :, slot]
        return s < 4, remote(src, w.at[:, :, slot], wr_s.at[k], wr_r.at[k], dev(x, y, up_z, c))

    def right_came(k):
        return (pos + 2 * NZ - k - 1) % NZ < 4

    def left(k):
        s = (pos + k) % NZ
        slot = s % 4
        src = wt_in if k == 0 else w.at[:, :, slot]
        return s < 4, remote(src, w.at[:, :, slot], wl_s.at[k], wl_r.at[k], dev(x, y, down_z, c))

    def left_came(k):
        return (pos + k + 1) % NZ < 4

    def start_if(pair):
        ok, copy = pair

        @pl.when(ok)
        def _():
            copy.start()

    def wait_recv_if(ok, copy):
        @pl.when(ok)
        def _():
            copy.wait_recv()

    def w_step(k):
        wait_recv_if(right_came(k), right(k)[1])
        if k < 3:
            start_if(right(k + 1))
            wait_recv_if(left_came(k), left(k)[1])
            if k < 2:
                start_if(left(k + 1))

    start_if(right(0))
    start_if(left(0))
    for i in range(5):
        gather(0, i).start()
    for i in range(5):
        gather(1, i).start()
    own = [
        pltpu.make_async_copy(og_in, block(og, y, c), loc_s.at[0]),
        pltpu.make_async_copy(lat_in, block(xg, y, c), loc_s.at[1]),
    ]
    own_w = pltpu.make_async_copy(wt_in, w.at[:, :, pos % 4], loc_s.at[2])
    for copy in own:
        copy.start()

    @pl.when(pos < 4)
    def _():
        own_w.start()

    w2_copies = []
    for a in range(3):
        for s in range(4):
            first = 32 * (yhi * NZ + 4 * c + s) + 16 * ylo
            w2_copies.append(pltpu.make_async_copy(
                w2_in.at[pl.ds(9 * a, 9), pl.ds(pl.multiple_of(first, 16), 16)],
                w2.at[:, a, s], w2_s.at[a, s],
            ))
    for copy in w2_copies:
        copy.start()

    acc[...] = jnp.zeros_like(acc)
    q[...] = jnp.zeros_like(q)
    gi[...] = jnp.zeros_like(gi)

    for n in range(2):
        gather(n, 0).wait_recv()
        gather(n, 5).start()
        gather(n, 1).wait_recv()
        gather(n, 6).start()
    w_step(0)
    for n in range(2):
        gather(n, 2).wait_recv()
        gather(n, 7).start()
        gather(n, 3).wait_recv()
        gather(n, 8).start()
    w_step(1)
    for n in range(2):
        gather(n, 5).wait_recv()
        gather(n, 6).wait_recv()
        gather(n, 9).start()
    w_step(2)
    own[0].wait()
    for i in (4, 7, 8, 9):
        gather(0, i).wait_recv()

    def sum_step(i, _):
        f, band = i // 2, i % 2
        part = dot(sums_in[...], og[f, band], NN)
        for k in range(9):
            g[k, f, band] = part[64 * k : 64 * k + 64].astype(BF)
        for k in range(6):
            gh[k, f, band] = part[576 + 16 * k : 592 + 16 * k].astype(BF)
        return 0

    lax.fori_loop(0, 16, sum_step, 0)

    for copy in w2_copies:
        copy.wait()

    def q_step(k, _):
        wk = w2[k].reshape(192, 256)
        q[...] += dot(g[k].reshape(1024, 256), wk, NT).reshape(8, 2, 64, 192)
        return 0

    lax.fori_loop(0, 9, q_step, 0)
    for side in range(2):
        total = None
        for e in range(3):
            wk = w2[6 * side + e].reshape(192, 256)
            term = dot(gh[3 * side + e].reshape(256, 256), wk, NT)
            total = term if total is None else total + term
        qh[side] = total.reshape(8, 2, 16, 192)

    def through_time(ref, t):
        out = ref[t, :, :, 128:192]
        if t < 7:
            out = out + ref[t + 1, :, :, 64:128]
        if t < 6:
            out = out + ref[t + 2, :, :, 0:64]
        return out

    for t in range(8):
        ga[t] = through_time(q, t)

    w_step(3)

    @pl.when(pos < 4)
    def _():
        own_w.wait()

    own[1].wait()
    for i in (4, 7, 8, 9):
        gather(1, i).wait_recv()

    for a in range(3):
        n = 6 + a
        for b in range(3):
            part = dot(xg[0:n].reshape(n * 128, 512), w[3 * a + b].reshape(192, 512), NT)
            acc[2 - a : 8, :, 16 * (2 - b) : 16 * (2 - b) + 64, :] += part.reshape(n, 2, 64, 192)

    col96 = lax.broadcasted_iota(jnp.int32, (192, 64), 0) % 16

    def columns(t, _):
        part = acc[t].reshape(192, 192)
        before = jnp.where(col96 == 0, 0.0, pltpu.roll(part[:, 0:64], 1, 0))
        after = jnp.where(col96 == 15, 0.0, pltpu.roll(part[:, 128:192], 191, 0))
        pre[t] = (before + part[:, 64:128] + after).reshape(2, 96, 64)
        return 0

    lax.fori_loop(0, 8, columns, 0)

    for t in range(8):
        for side in range(2):
            rim = pre[t, :, 80 * side : 80 * side + 16]
            e1s[side, t] = jnp.concatenate([rim, through_time(qh.at[side], t)], axis=-1).astype(BF)

    def edge_copy(src, dst, base, side):
        target = dev(x, y, down_z if side == 0 else up_z, c)
        return remote(src.at[side], dst.at[side], e_s.at[base, side], e_r.at[base, side], target)

    for side in range(2):
        edge_copy(e1s, e1r, 0, side).start()
    for side in range(2):
        edge_copy(e1s, e1r, 0, side).wait_recv()

    last, first = z == NZ - 1, z == 0

    def from_below(v):
        return jnp.where(last, jnp.stack([v[1], jnp.zeros_like(v[1])]), v)

    def from_above(v):
        return jnp.where(first, jnp.stack([jnp.zeros_like(v[0]), v[0]]), v)

    for t in range(8):
        below = from_below(e1r[0, t].astype(F32))
        above = from_above(e1r[1, t].astype(F32))
        zero = jnp.zeros((2, 32, 128), F32)
        both = jnp.concatenate([above, zero, below], axis=1)
        v = pre[t, :, 16:80] + both[:, :, 0:64]
        d = ga[t] + both[:, :, 64:128]
        s = 1.0 / (1.0 + jnp.exp(-v))
        a_now = v * s
        p_now = d * (s * (1.0 + v * (1.0 - s)))
        act[t] = a_now
        pre[t, :, 16:80] = p_now
        pair = jnp.concatenate([a_now, p_now], axis=-1).astype(BF)
        e2s[0, t] = pair[:, 0:16]
        e2s[1, t] = pair[:, 48:64]

    for side in range(2):
        edge_copy(e2s, e2r, 1, side).start()

    def stacked(ref, t):
        v = ref[t]
        zero = jnp.zeros_like(v)
        return jnp.concatenate([ref[t - 2] if t > 1 else zero, ref[t - 1] if t > 0 else zero, v], axis=-1)

    for t in range(8):
        act3[t] = stacked(act, t).astype(BF)
    act3t[...] = dot(eye_in[...], act3[...].reshape(1024, 192), NT).astype(BF)

    for side in range(2):
        edge_copy(e2s, e2r, 1, side).wait_recv()

    for t in range(8):
        below = from_below(e2r[0, t].astype(F32))
        above = from_above(e2r[1, t].astype(F32))
        pre[t, :, 0:16] = above[:, :, 64:128]
        pre[t, :, 80:96] = below[:, :, 64:128]
        qh[0, t, :, :, 0:64] = above[:, :, 0:64]
        qh[1, t, :, :, 0:64] = below[:, :, 0:64]
    for side in range(2):
        rows = []
        for t in range(8):
            v = qh[side, t, :, :, 0:64]
            zero = jnp.zeros_like(v)
            rows.append(jnp.concatenate([
                qh[side, t - 2, :, :, 0:64] if t > 1 else zero,
                qh[side, t - 1, :, :, 0:64] if t > 0 else zero, v], axis=-1).reshape(32, 192))
        stack = jnp.concatenate(rows, axis=0).astype(BF)
        hal3t[side] = dot(eye_in[...], stack, NT).astype(BF)

    for k in range(9):
        part = dot(act3t[...], g[k].reshape(1024, 256), NN)
        if k // 3 != 1:
            side = k // 6
            part = part + dot(hal3t[side], gh[3 * side + k % 3].reshape(256, 256), NN)
        gws[k] = part.astype(BF).reshape(3, 4, 16, 256)

    def x_copy(d):
        to = (x + d) % 4
        return remote(gws.at[:, :, to], ra.at[d - 1], a_s.at[d - 1], a_r.at[d - 1], dev(to, y, z, c))

    for d in range(1, 4):
        x_copy(d).start()

    def shifted(t, _):
        part = pre[t].reshape(192, 64)
        after = jnp.where(col96 == 15, 0.0, pltpu.roll(part, 191, 0))
        before = jnp.where(col96 == 0, 0.0, pltpu.roll(part, 1, 0))
        gp3[t] = jnp.concatenate([after, part, before], axis=-1).reshape(2, 96, 192).astype(BF)
        return 0

    lax.fori_loop(0, 8, shifted, 0)
    for a in range(3):
        n = 6 + a
        for b in range(3):
            rows = gp3[2 - a : 8, :, 16 * (2 - b) : 16 * (2 - b) + 64, :].reshape(n * 128, 192)
            part = dot(rows, w[3 * a + b].reshape(192, 512), NN)
            gi[0:n] += part.reshape(n, 2, 64, 512)

    for half in range(2):
        for f in range(2):
            pb[half, f] = gi[4 * half + 2 * (1 - c) + f].astype(BF)
    pair_copy = remote(pb, rp, pr_s, pr_r, dev(x, y, z, 1 - c))
    pair_copy.start()

    for d in range(1, 4):
        x_copy(d).wait_recv()

    def x_sum(k, _):
        total = gws[k, :, x].astype(F32)
        for d in range(3):
            total = total + ra[d, k].astype(F32)
        sb[pl.ds(3 * k, 3)] = total.astype(BF)
        return 0

    lax.fori_loop(0, 9, x_sum, 0)
    sb[27:32] = jnp.zeros((5, 16, 256), BF)

    def z_copy(d):
        to = (z + d) % NZ
        return remote(sb.at[pl.ds(4 * to, 4)], rb.at[d - 1], b_s.at[d - 1], b_r.at[d - 1], dev(x, y, to, c))

    for d in range(1, NZ):
        z_copy(d).start()

    pair_copy.wait_recv()
    for half in range(2):
        for f in range(2):
            ps[half, f] = (gi[4 * half + 2 * c + f] + rp[half, f].astype(F32)).astype(BF)

    def y_copy(d):
        to = (y + d) % 4
        return remote(ps.at[to % 2, :, to // 2], rr.at[d - 1], rs_s.at[d - 1], rs_r.at[d - 1], dev(x, to, z, c))

    for d in range(1, 4):
        y_copy(d).start()

    for d in range(1, NZ):
        z_copy(d).wait_recv()
    total = sb[pl.ds(4 * z, 4)].astype(F32)
    for d in range(NZ - 1):
        total = total + rb[d].astype(F32)
    fc[...] = (total * scale).reshape(4, 2, 8, 256)

    def out_copy(to_x, half):
        target = dev(to_x, y_own, z_own + half, c)
        return remote(fc.at[:, half], rc.at[z], c_s.at[to_x, half], c_r.at[z], target)

    def out_self(half):
        return pltpu.make_async_copy(fc.at[:, half], rc.at[z], c_r.at[z])

    for half in range(2):
        for to_x in range(4):
            mine = jnp.logical_and(jnp.logical_and(x == to_x, y == y_own), z == z_own + half)

            @pl.when(mine)
            def _():
                out_self(half).start()

            @pl.when(jnp.logical_not(mine))
            def _():
                out_copy(to_x, half).start()

    for d in range(1, 4):
        y_copy(d).wait_recv()
    total = ps[ylo, :, yhi].astype(F32)
    for d in range(3):
        total = total + rr[d].astype(F32)
    gi_out[...] = total.astype(BF)

    for s in range(NZ):
        pltpu.make_async_copy(rc.at[s], rc.at[s], c_r.at[s]).wait()
    gw_out[...] = rc[...].reshape(32, 8, 256)

    for n in range(2):
        for i in range(10):
            gather(n, i).wait_send()
    for k in range(4):
        ok, copy = right(k)

        @pl.when(ok)
        def _():
            copy.wait_send()
    for k in range(3):
        ok, copy = left(k)

        @pl.when(ok)
        def _():
            copy.wait_send()
    for side in range(2):
        edge_copy(e1s, e1r, 0, side).wait_send()
        edge_copy(e2s, e2r, 1, side).wait_send()
    pair_copy.wait_send()
    for d in range(1, 4):
        x_copy(d).wait_send()
        y_copy(d).wait_send()
    for d in range(1, NZ):
        z_copy(d).wait_send()
    for half in range(2):
        for to_x in range(4):
            mine = jnp.logical_and(jnp.logical_and(x == to_x, y == y_own), z == z_own + half)

            @pl.when(jnp.logical_not(mine))
            def _():
                out_copy(to_x, half).wait_send()


def on_device(latent, out_grad, w_first, w_second):
    ylo = lax.axis_index("tm") // 2
    half = lax.dynamic_slice_in_dim(w_first, 16 * ylo, 16, axis=2)
    wt = jnp.swapaxes(half, 1, 2).reshape(9, 3, 16, 512)
    scale = 1.0 / math.sqrt(131072.0)
    hbm = pl.BlockSpec(memory_space=pl.ANY)
    vmem = pl.BlockSpec(memory_space=pltpu.VMEM)
    dma = pltpu.SemaphoreType.DMA
    grad_input, grad_w2 = pl.pallas_call(
        functools.partial(body, scale),
        out_shape=(
            jax.ShapeDtypeStruct((2, 64, 512), BF),
            jax.ShapeDtypeStruct((32, 8, 256), F32),
        ),
        in_specs=[hbm, hbm, hbm, hbm, vmem, vmem],
        out_specs=(vmem, vmem),
        scratch_shapes=[
            pltpu.VMEM((8, 2, 64, 512), BF),
            pltpu.VMEM((8, 2, 256, 256), BF),
            pltpu.VMEM((9, 3, 4, 16, 512), BF),
            pltpu.VMEM((9, 3, 4, 16, 256), BF),
            pltpu.VMEM((9, 8, 2, 64, 256), BF),
            pltpu.VMEM((6, 8, 2, 16, 256), BF),
            pltpu.VMEM((8, 2, 96, 192), F32),
            pltpu.VMEM((8, 2, 64, 192), F32),
            pltpu.VMEM((2, 8, 2, 16, 192), F32),
            pltpu.VMEM((8, 2, 96, 64), F32),
            pltpu.VMEM((8, 2, 64, 64), F32),
            pltpu.VMEM((2, 8, 2, 16, 128), BF),
            pltpu.VMEM((2, 8, 2, 16, 128), BF),
            pltpu.VMEM((2, 8, 2, 16, 128), BF),
            pltpu.VMEM((2, 8, 2, 16, 128), BF),
            pltpu.VMEM((8, 2, 64, 64), F32),
            pltpu.VMEM((8, 2, 96, 192), BF),
            pltpu.VMEM((8, 2, 64, 192), BF),
            pltpu.VMEM((192, 1024), BF),
            pltpu.VMEM((2, 192, 256), BF),
            pltpu.VMEM((8, 2, 64, 512), F32),
            pltpu.VMEM((2, 2, 2, 64, 512), BF),
            pltpu.VMEM((2, 2, 2, 64, 512), BF),
            pltpu.VMEM((2, 2, 2, 64, 512), BF),
            pltpu.VMEM((3, 2, 64, 512), BF),
            pltpu.VMEM((9, 3, 4, 16, 256), BF),
            pltpu.VMEM((3, 9, 3, 16, 256), BF),
            pltpu.VMEM((32, 16, 256), BF),
            pltpu.VMEM((7, 4, 16, 256), BF),
            pltpu.VMEM((4, 2, 8, 256), F32),
            pltpu.VMEM((8, 4, 8, 256), F32),
            dma((2, 10)), dma((2, 10)),
            dma((4,)), dma((4,)), dma((3,)), dma((3,)),
            dma((3, 4)), dma((3,)),
            dma((2, 2)), dma((2, 2)),
            dma, dma,
            dma((3,)), dma((3,)),
            dma((3,)), dma((3,)),
            dma((7,)), dma((7,)),
            dma((4, 2)), dma((8,)),
        ],
        compiler_params=pltpu.CompilerParams(
            collective_id=0, has_side_effects=True, vmem_limit_bytes=56 * 1024 * 1024
        ),
    )(
        latent.reshape(2, 64, 512),
        out_grad.reshape(2, 256, 256),
        wt,
        w_second,
        jnp.asarray(cell_sums(), BF),
        jnp.asarray(np.eye(192, dtype=np.float32), BF),
    )
    grad_w2 = grad_w2[:27].reshape(9, 3, 8, 256).transpose(2, 1, 0, 3).reshape(8, 27, 256)
    return grad_input.reshape(1, 2, 4, 16, 512), grad_w2


def solution(mesh):
    placed = (
        P("dp", "tm", "height", None, None),
        P("dp", "tm", "height", None, None),
        P(None, None, "height"),
        P(),
    )
    return jax.shard_map(
        on_device,
        mesh=mesh,
        in_specs=placed,
        out_specs=(P("dp", "tm", "height", None, None), P(("tm", "height"), None, None)),
        check_vma=False,
    )
```

time: 664 us -> 98 us (0.15)
  the two profiles are of different devices: /device:TPU:8 before, /device:TPU:110 now
where the time goes in v1:
time: 98 us; the launch traced here: 97.8 us
  Pallas kernels  92 us (94%)
  local copies, waits for them, and re-layouts  5.17 us (5%)
    pallas_call x1, Pallas kernels, on_device(): pl.pallas_call(functools.partial(body, scale), out_shape=(jax.ShapeDtypeS...  92 us
    unnamed x3, local copies, waits for them, and re-layouts  2.72 us

profile of v1, /device:TPU:110, one launch (start us, length us, event | category | flops | bytes accessed | tf_op | source)
XLA Modules:
  0.0 97.8 jit_solution(14576172282388292125)
XLA Ops:
  0.6 0.0 copy-start
  0.7 1.1 %copy-done = bf16[27,512,32]{1,2,0:T(8,128)(2,1)S(1)} copy-done((bf16[27,512,32]{1,2,0:T(8,128)(2,1)S(1)}, bf16[27,512,32]{1,2,0:T(8,128)(2,1)}, u32[]{:S(2)}) %copy-start) | copy-done | bytes 884760
  1.8 0.8 constant_dynamic-slice_fusion
  2.6 92.0 %shard_map.77 = (bf16[2,64,512]{2,1,0:T(8,128)(2,1)}, f32[32,8,256]{2,1,0:T(8,128)}) custom-call(bf16[2,64,512]{2,1,0:T(8,128)(2,1)} %bitcast.14, bf16[2,256,256]{2,1,0:T(8,128)(2,1)} %bitcast.12, bf16[9,3,16,512]{3,2,1,0:T(8,128)(2,1)} %bitcast.10, bf16[27,512,256]{2,1,0:T(8,128)(2,1)} %w2_in.1, bf16[672,256]{1,0:T(8,128)(2,1)} %constant.29.clone.sums_in, ...), custom_call_target="tpu_custom_call" | custom-call | tf_op jit(solution)/shard_map/pallas_call | solution.py:503
  94.6 1.0 slice.3
  95.6 0.7 copy.8
  96.3 1.6 %copy.10 = bf16[1,2,4,16,512]{4,3,2,1,0:T(8,128)(2,1)} copy(bf16[1,2,4,16,512]{4,3,2,1,0:T(8,128)(2,1)} %bitcast.15) | data formatting | bytes 262144
Async XLA Ops:
  0.6 1.2 %copy-start = (bf16[27,512,32]{1,2,0:T(8,128)(2,1)S(1)}, bf16[27,512,32]{1,2,0:T(8,128)(2,1)}, u32[]{:S(2)}) copy-start(bf16[27,512,32]{1,2,0:T(8,128)(2,1)} %param.8) | copy-start | bytes 2654212

commit v2 on v1

v2 whole, which is shorter than its diff:
```python
import functools
import math

import jax
import jax.numpy as jnp
import numpy as np
from jax import lax
from jax.experimental import pallas as pl
from jax.experimental.pallas import tpu as pltpu
from jax.sharding import PartitionSpec as P

MESH = pl.DeviceIdType.MESH
BF = jnp.bfloat16
F32 = jnp.float32
NZ = 8
NT = (((1,), (1,)), ((), ()))
NN = (((1,), (0,)), ((), ()))


def cell_sums():
    main = np.zeros((3, 3, 4, 16, 8, 32), np.float32)
    edge = np.zeros((2, 3, 16, 8, 32), np.float32)
    for b in range(3):
        for e in range(3):
            for c in range(16):
                cols = [2 * c + q + 1 - e for q in range(2) if 0 <= 2 * c + q + 1 - e < 32]
                for h in range(4):
                    for p in range(2):
                        row = 2 * h + p + 1 - b
                        if 0 <= row < 8:
                            main[b, e, h, c, row, cols] = 1.0
                if b == 0:
                    edge[0, e, c, 0, cols] = 1.0
                if b == 2:
                    edge[1, e, c, 7, cols] = 1.0
    return np.concatenate([main.reshape(576, 256), edge.reshape(96, 256)], axis=0)


def dot(a, b, dims):
    return lax.dot_general(a, b, dims, preferred_element_type=F32)


def body(
    scale,
    lat_in, og_in, wt_in, w2_in, sums_in, eye_in,
    gi_out, gw_out,
    xg, og, w, w2, g, gh, acc, q, qh, pre, ga, es, er,
    act, gp3, act3, act3t, hal3t, gi, pb, rp, ps, rr, gws, ra, sbf, sb, rb, fc, rc,
    loc_s, ag_s, ag_r, wz_s, wz_r, wx_s, wx_r, e_s, e_r, pr_s, pr_r, rs_s, rs_r,
    a_s, a_r, b_s, b_r, c_s, c_r,
):
    x = lax.axis_index("dp")
    tm = lax.axis_index("tm")
    height = lax.axis_index("height")
    c = tm % 2
    ylo = tm // 2
    z = height % NZ
    yhi = height // NZ
    y = 2 * yhi + ylo
    y_out = 2 * ylo + yhi

    def dev(x_, y_, z_, c_):
        return (x_, (y_ % 2) * 2 + c_, (y_ // 2) * NZ + z_)

    up_y, down_y = (y + 1) % 4, (y + 3) % 4
    up_z, down_z = (z + 1) % NZ, (z + NZ - 1) % NZ
    up_x, down_x = (x + 1) % 4, (x + 3) % 4
    far_y, far_x = (y + 2) % 4, (x + 2) % 4

    def remote(src, dst, ssem, rsem, target):
        return pltpu.make_async_remote_copy(
            src_ref=src, dst_ref=dst, send_sem=ssem, recv_sem=rsem,
            device_id=target, device_id_type=MESH,
        )

    def slab(ref, y_, c_, f):
        return ref.at[2 * (2 * (y_ % 2) + c_) + f, y_ // 2]

    def block(ref, y_, c_):
        return ref.at[pl.ds(2 * (2 * (y_ % 2) + c_), 2), y_ // 2]

    pos = (z + NZ - (4 * c + 2 * ylo)) % NZ
    source = pos < 2
    base = 64 * (4 * yhi + 2 * c + ylo)
    own = [
        pltpu.make_async_copy(lat_in, block(xg, y, c), loc_s.at[0]),
        pltpu.make_async_copy(og_in, block(og, y, c), loc_s.at[1]),
    ]
    own_w = pltpu.make_async_copy(wt_in, w.at[:, pos % 2], loc_s.at[2])
    w2_copies = [
        pltpu.make_async_copy(
            w2_in.at[pl.ds(9 * a, 9), pl.ds(pl.multiple_of(base, 64), 64)], w2.at[:, a], loc_s.at[3 + a]
        )
        for a in range(3)
    ]

    @pl.when(source)
    def _():
        own_w.start()

    for copy in own:
        copy.start()

    barrier = pltpu.get_barrier_semaphore()

    def greet(target):
        pl.semaphore_signal(barrier, inc=1, device_id=target, device_id_type=MESH)

    greet(dev(x, y, z, 1 - c))
    for d in (1, 3, 2):
        greet(dev(x, (y + d) % 4, z, c))
        greet(dev((x + d) % 4, y, z, c))
    for d in (1, 7, 2, 6, 3, 5, 4):
        greet(dev(x, y, (z + d) % NZ, c))
    swaps = y != y_out

    @pl.when(swaps)
    def _():
        for d in range(1, 4):
            greet(dev((x + d) % 4, y_out, z, c))

    for copy in w2_copies:
        copy.start()
    acc[...] = jnp.zeros_like(acc)

    @pl.when(source)
    def _():
        own_w.wait()

    for copy in own:
        copy.wait()
    pl.semaphore_wait(barrier, 14 + 3 * swaps.astype(jnp.int32))

    arrays = (xg, og)

    def gather(n, i):
        ref = arrays[n]
        up, down, mate = dev(x, up_y, z, c), dev(x, down_y, z, c), dev(x, y, z, 1 - c)
        place, target = {
            0: lambda: (slab(ref, y, c, 0), up),
            1: lambda: (slab(ref, y, c, 1), down),
            2: lambda: (slab(ref, y, c, 1), up),
            3: lambda: (slab(ref, y, c, 0), down),
            4: lambda: (block(ref, y, c), mate),
            5: lambda: (slab(ref, down_y, c, 0), up),
            6: lambda: (slab(ref, up_y, c, 1), down),
            7: lambda: (block(ref, down_y, c), mate),
            8: lambda: (block(ref, up_y, c), mate),
            9: lambda: (block(ref, far_y, c), mate),
        }[i]()
        return remote(place, place, ag_s.at[n, i], ag_r.at[n, i], target)

    reach = (4, 3)

    def share(part, slot):
        if part == 0:
            return w.at[pl.ds(4 * x, 4), slot]
        return w.at[16:27, slot]

    def along_z(part, slot, way):
        target = dev(x, y, up_z if way == 0 else down_z, c)
        place = share(part, slot)
        return remote(place, place, wz_s.at[part, slot, way], wz_r.at[part, slot], target)

    def z_sends(part, slot, act_on):
        far = (pos + NZ - slot) % NZ
        r = reach[part]

        @pl.when(far < r)
        def _():
            act_on(along_z(part, slot, 0))

        @pl.when(jnp.logical_or(far == 0, far > r + 1))
        def _():
            act_on(along_z(part, slot, 1))

    def z_recv(part, slot):
        @pl.when(pos != slot)
        def _():
            along_z(part, slot, 0).wait_recv()

    def along_x(slot, i):
        up, down = dev(up_x, y, z, c), dev(down_x, y, z, c)
        first, target = {
            0: lambda: (4 * x, up),
            1: lambda: (4 * x, down),
            2: lambda: (4 * down_x, up),
            3: lambda: (4 * up_x + 2, down),
        }[i]()
        place = w.at[pl.ds(first, 4 if i < 2 else 2), slot]
        return remote(place, place, wx_s.at[slot, i], wx_r.at[slot, i], target)

    def start(copy):
        copy.start()

    near = jnp.where(jnp.logical_and(pos >= 1, pos <= 4), 1, 0)
    slots = (near, 1 - near)
    own_slot = pos % 2

    @pl.when(source)
    def _():
        z_sends(0, own_slot, start)

    for i in range(5):
        gather(0, i).start()

    @pl.when(source)
    def _():
        z_sends(1, own_slot, start)

    for i in range(5):
        gather(1, i).start()

    def pass_on(part, slot):
        @pl.when(pos != slot)
        def _():
            along_z(part, slot, 0).wait_recv()
            z_sends(part, slot, start)
            if part == 0:
                along_x(slot, 0).start()
                along_x(slot, 1).start()

    def pass_x(slot):
        @pl.when(pos != slot)
        def _():
            along_x(slot, 0).wait_recv()
            along_x(slot, 2).start()
            along_x(slot, 1).wait_recv()
            along_x(slot, 3).start()

    def pass_y(n):
        gather(n, 0).wait_recv()
        gather(n, 5).start()
        gather(n, 1).wait_recv()
        gather(n, 6).start()

    def pass_mate(n):
        gather(n, 2).wait_recv()
        gather(n, 7).start()
        gather(n, 3).wait_recv()
        gather(n, 8).start()

    def pass_far(n):
        gather(n, 5).wait_recv()
        gather(n, 6).wait_recv()
        gather(n, 9).start()

    pass_on(0, slots[0])
    pass_y(0)
    pass_on(0, slots[1])
    pass_mate(0)
    pass_x(slots[0])
    pass_on(1, slots[0])
    pass_y(1)
    pass_far(0)
    pass_x(slots[1])
    pass_on(1, slots[1])
    pass_mate(1)
    pass_far(1)

    for i in (4, 7, 8, 9):
        gather(0, i).wait_recv()
    for slot in range(2):
        @pl.when(pos != slot)
        def _():
            along_x(slot, 2).wait_recv()
            along_x(slot, 3).wait_recv()

    for a in range(3):
        n = 6 + a
        for b in range(3):
            k = 9 * a + 3 * b
            part = dot(xg[0:n].reshape(n * 128, 512), w[k : k + 3].reshape(192, 512), NT)
            acc[2 - a : 8, :, 16 * (2 - b) : 16 * (2 - b) + 64, :] += part.reshape(n, 2, 64, 192)

    col96 = lax.broadcasted_iota(jnp.int32, (192, 64), 0) % 16

    def columns(t, _):
        part = acc[t].reshape(192, 192)
        before = jnp.where(col96 == 0, 0.0, pltpu.roll(part[:, 0:64], 1, 0))
        after = jnp.where(col96 == 15, 0.0, pltpu.roll(part[:, 128:192], 191, 0))
        pre[t] = (before + part[:, 64:128] + after).reshape(2, 96, 64)
        return 0

    lax.fori_loop(0, 8, columns, 0)

    def edge_copy(n, side):
        target = dev(x, y, down_z if side == 0 else up_z, c)
        return remote(es.at[n, side], er.at[n, side], e_s.at[n, side], e_r.at[n, side], target)

    def edge_send(n, rows):
        for side in range(2):
            for t in range(4):
                es[n, side, t] = jnp.concatenate([rows(side, t), rows(side, t + 4)], axis=-1).astype(BF)
            edge_copy(n, side).start()

    def edge_wait(n):
        for side in range(2):
            edge_copy(n, side).wait_recv()

    last, first = z == NZ - 1, z == 0

    def edge_rows(n, side, t):
        v = er[n, side, t % 4][:, :, 64 * (t // 4) : 64 * (t // 4) + 64].astype(F32)
        if side == 0:
            return jnp.where(last, jnp.stack([v[1], jnp.zeros_like(v[1])]), v)
        return jnp.where(first, jnp.stack([jnp.zeros_like(v[0]), v[0]]), v)

    edge_send(0, lambda side, t: pre[t, :, 80 * side : 80 * side + 16])

    for i in (4, 7, 8, 9):
        gather(1, i).wait_recv()

    def sum_step(i, _):
        f, band = i // 2, i % 2
        part = dot(sums_in[...], og[f, band], NN)
        for k in range(9):
            g[k, f, band] = part[64 * k : 64 * k + 64].astype(BF)
        for k in range(6):
            gh[k, f, band] = part[576 + 16 * k : 592 + 16 * k].astype(BF)
        return 0

    lax.fori_loop(0, 16, sum_step, 0)
    for copy in w2_copies:
        copy.wait()
    q[...] = jnp.zeros_like(q)

    def q_step(k, _):
        wk = w2[k].reshape(192, 256)
        q[...] += dot(g[k].reshape(1024, 256), wk, NT).reshape(8, 2, 64, 192)
        return 0

    lax.fori_loop(0, 9, q_step, 0)
    for side in range(2):
        total = None
        for e in range(3):
            wk = w2[6 * side + e].reshape(192, 256)
            term = dot(gh[3 * side + e].reshape(256, 256), wk, NT)
            total = term if total is None else total + term
        qh[side] = total.reshape(8, 2, 16, 192)

    def through_time(ref, t):
        out = ref[t, :, :, 128:192]
        if t < 7:
            out = out + ref[t + 1, :, :, 64:128]
        if t < 6:
            out = out + ref[t + 2, :, :, 0:64]
        return out

    edge_send(1, lambda side, t: through_time(qh.at[side], t))
    for t in range(8):
        ga[t] = through_time(q, t)

    edge_wait(0)
    for t in range(8):
        pre[t, :, 16:32] += edge_rows(0, 1, t)
        pre[t, :, 64:80] += edge_rows(0, 0, t)
        v = pre[t, :, 16:80]
        s = 1.0 / (1.0 + jnp.exp(-v))
        act[t] = v * s
        pre[t, :, 16:80] = s * (1.0 + v * (1.0 - s))
    edge_send(2, lambda side, t: act[t, :, 48 * side : 48 * side + 16])

    def stacked(rows, t):
        v = rows(t)
        zero = jnp.zeros_like(v)
        return jnp.concatenate([rows(t - 2) if t > 1 else zero, rows(t - 1) if t > 0 else zero, v], axis=-1)

    for t in range(8):
        act3[t] = stacked(lambda u: act[u], t).astype(BF)
    act3t[...] = dot(eye_in[...], act3[...].reshape(1024, 192), NT).astype(BF)

    edge_wait(1)
    for t in range(8):
        ga[t, :, 0:16] += edge_rows(1, 1, t)
        ga[t, :, 48:64] += edge_rows(1, 0, t)
        pre[t, :, 16:80] = ga[t] * pre[t, :, 16:80]
    edge_send(3, lambda side, t: pre[t, :, 16 + 48 * side : 32 + 48 * side])

    edge_wait(2)
    for t in range(8):
        for side in range(2):
            qh[side, t, :, :, 0:64] = edge_rows(2, 1 - side, t)
    for side in range(2):
        stack = jnp.concatenate(
            [stacked(lambda u: qh[side, u, :, :, 0:64], t).reshape(32, 192) for t in range(8)], axis=0
        ).astype(BF)
        hal3t[side] = dot(eye_in[...], stack, NT).astype(BF)

    for k in range(9):
        part = dot(act3t[...], g[k].reshape(1024, 256), NN)
        if k // 3 != 1:
            side = k // 6
            part = part + dot(hal3t[side], gh[3 * side + k % 3].reshape(256, 256), NN)
        gws[3 * k : 3 * k + 3] = part.astype(BF).reshape(3, 64, 256)
    gws[27] = jnp.zeros((64, 256), BF)

    def x_copy(d):
        to = (x + d) % 4
        return remote(gws.at[pl.ds(7 * to, 7)], ra.at[d - 1], a_s.at[d - 1], a_r.at[d - 1], dev(to, y, z, c))

    for d in (2, 1, 3):
        x_copy(d).start()

    edge_wait(3)
    for t in range(8):
        pre[t, :, 0:16] = edge_rows(3, 1, t)
        pre[t, :, 80:96] = edge_rows(3, 0, t)

    def shifted(t, _):
        part = pre[t].reshape(192, 64)
        after = jnp.where(col96 == 15, 0.0, pltpu.roll(part, 191, 0))
        before = jnp.where(col96 == 0, 0.0, pltpu.roll(part, 1, 0))
        gp3[t] = jnp.concatenate([after, part, before], axis=-1).reshape(2, 96, 192).astype(BF)
        return 0

    lax.fori_loop(0, 8, shifted, 0)
    gi[...] = jnp.zeros_like(gi)
    for a in range(3):
        n = 6 + a
        for b in range(3):
            k = 9 * a + 3 * b
            rows = gp3[2 - a : 8, :, 16 * (2 - b) : 16 * (2 - b) + 64, :].reshape(n * 128, 192)
            part = dot(rows, w[k : k + 3].reshape(192, 512), NN)
            gi[0:n] += part.reshape(n, 2, 64, 512)

    for half in range(2):
        for f in range(2):
            pb[half, f] = gi[4 * half + 2 * (1 - c) + f].astype(BF)
    pair_copy = remote(pb, rp, pr_s, pr_r, dev(x, y, z, 1 - c))
    pair_copy.start()

    for d in range(1, 4):
        x_copy(d).wait_recv()

    def x_sum(j, _):
        total = gws[7 * x + j].astype(F32)
        for d in range(3):
            total = total + ra[d, j].astype(F32)
        sbf[:, pl.ds(pl.multiple_of(8 * j, 8), 8)] = total.reshape(8, 8, 256)
        return 0

    lax.fori_loop(0, 7, x_sum, 0)
    sbf[:, 56:64] = jnp.zeros((8, 8, 256), F32)
    sb[...] = sbf[...].astype(BF)

    def z_copy(d):
        to = (z + d) % NZ
        return remote(sb.at[to], rb.at[d - 1], b_s.at[d - 1], b_r.at[d - 1], dev(x, y, to, c))

    for d in (4, 3, 5, 2, 6, 1, 7):
        z_copy(d).start()

    pair_copy.wait_recv()
    for half in range(2):
        for f in range(2):
            ps[half, f] = (gi[4 * half + 2 * c + f] + rp[half, f].astype(F32)).astype(BF)

    def y_copy(d):
        to = (y + d) % 4
        return remote(ps.at[to % 2, :, to // 2], rr.at[d - 1], rs_s.at[d - 1], rs_r.at[d - 1], dev(x, to, z, c))

    for d in (2, 1, 3):
        y_copy(d).start()

    for d in range(1, NZ):
        z_copy(d).wait_recv()
    total = sb[z].astype(F32)
    for d in range(NZ - 1):
        total = total + rb[d].astype(F32)
    fc[...] = (total * scale).astype(BF)

    def out_copy(to_x):
        return remote(fc, rc.at[x], c_s.at[to_x], c_r.at[x], dev(to_x, y_out, z, c))

    for to_x in range(4):
        mine = jnp.logical_and(x == to_x, y == y_out)

        @pl.when(mine)
        def _():
            pltpu.make_async_copy(fc, rc.at[x], c_r.at[x]).start()

        @pl.when(jnp.logical_not(mine))
        def _():
            out_copy(to_x).start()

    for d in range(1, 4):
        y_copy(d).wait_recv()
    total = ps[ylo, :, yhi].astype(F32)
    for d in range(3):
        total = total + rr[d].astype(F32)
    gi_out[...] = total.astype(BF)

    for part in range(4):
        pltpu.make_async_copy(fc, rc.at[part], c_r.at[part]).wait()
        v = rc[part].astype(F32)
        for j in range(7):
            k, a = (7 * part + j) // 3, (7 * part + j) % 3
            if k < 9:
                gw_out[9 * a + k] = v[8 * j : 8 * j + 8]

    def sent(copy):
        copy.wait_send()

    for n in range(2):
        for i in range(10):
            gather(n, i).wait_send()
        for slot in range(2):
            z_sends(n, slot, sent)
    for slot in range(2):
        @pl.when(pos != slot)
        def _():
            for i in range(4):
                along_x(slot, i).wait_send()

    for n in range(4):
        for side in range(2):
            edge_copy(n, side).wait_send()
    pair_copy.wait_send()
    for d in range(1, 4):
        x_copy(d).wait_send()
        y_copy(d).wait_send()
    for d in range(1, NZ):
        z_copy(d).wait_send()
    for to_x in range(4):
        @pl.when(jnp.logical_not(jnp.logical_and(x == to_x, y == y_out)))
        def _():
            out_copy(to_x).wait_send()


def on_device(latent, out_grad, w_first, w_second):
    wt = jnp.swapaxes(w_first, 1, 2)
    scale = 1.0 / math.sqrt(131072.0)
    hbm = pl.BlockSpec(memory_space=pl.ANY)
    vmem = pl.BlockSpec(memory_space=pltpu.VMEM)
    dma = pltpu.SemaphoreType.DMA
    grad_input, grad_w2 = pl.pallas_call(
        functools.partial(body, scale),
        out_shape=(
            jax.ShapeDtypeStruct((2, 64, 512), BF),
            jax.ShapeDtypeStruct((27, 8, 256), F32),
        ),
        in_specs=[hbm, hbm, hbm, hbm, vmem, vmem],
        out_specs=(vmem, vmem),
        scratch_shapes=[
            pltpu.VMEM((8, 2, 64, 512), BF),
            pltpu.VMEM((8, 2, 256, 256), BF),
            pltpu.VMEM((27, 2, 32, 512), BF),
            pltpu.VMEM((9, 3, 64, 256), BF),
            pltpu.VMEM((9, 8, 2, 64, 256), BF),
            pltpu.VMEM((6, 8, 2, 16, 256), BF),
            pltpu.VMEM((8, 2, 96, 192), F32),
            pltpu.VMEM((8, 2, 64, 192), F32),
            pltpu.VMEM((2, 8, 2, 16, 192), F32),
            pltpu.VMEM((8, 2, 96, 64), F32),
            pltpu.VMEM((8, 2, 64, 64), F32),
            pltpu.VMEM((4, 2, 4, 2, 16, 128), BF),
            pltpu.VMEM((4, 2, 4, 2, 16, 128), BF),
            pltpu.VMEM((8, 2, 64, 64), F32),
            pltpu.VMEM((8, 2, 96, 192), BF),
            pltpu.VMEM((8, 2, 64, 192), BF),
            pltpu.VMEM((192, 1024), BF),
            pltpu.VMEM((2, 192, 256), BF),
            pltpu.VMEM((8, 2, 64, 512), F32),
            pltpu.VMEM((2, 2, 2, 64, 512), BF),
            pltpu.VMEM((2, 2, 2, 64, 512), BF),
            pltpu.VMEM((2, 2, 2, 64, 512), BF),
            pltpu.VMEM((3, 2, 64, 512), BF),
            pltpu.VMEM((28, 64, 256), BF),
            pltpu.VMEM((3, 7, 64, 256), BF),
            pltpu.VMEM((8, 64, 256), F32),
            pltpu.VMEM((8, 64, 256), BF),
            pltpu.VMEM((7, 64, 256), BF),
            pltpu.VMEM((64, 256), BF),
            pltpu.VMEM((4, 64, 256), BF),
            dma((6,)),
            dma((2, 10)), dma((2, 10)),
            dma((2, 2, 2)), dma((2, 2)),
            dma((2, 4)), dma((2, 4)),
            dma((4, 2)), dma((4, 2)),
            dma, dma,
            dma((3,)), dma((3,)),
            dma((3,)), dma((3,)),
            dma((7,)), dma((7,)),
            dma((4,)), dma((4,)),
        ],
        compiler_params=pltpu.CompilerParams(
            collective_id=0, has_side_effects=True, vmem_limit_bytes=56 * 1024 * 1024
        ),
    )(
        latent.reshape(2, 64, 512),
        out_grad.reshape(2, 256, 256),
        wt,
        w_second,
        jnp.asarray(cell_sums(), BF),
        jnp.asarray(np.eye(192, dtype=np.float32), BF),
    )
    return grad_input.reshape(1, 2, 4, 16, 512), jnp.swapaxes(grad_w2, 0, 1)


def solution(mesh):
    placed = (
        P("dp", "tm", "height", None, None),
        P("dp", "tm", "height", None, None),
        P(None, None, "height"),
        P(),
    )
    return jax.shard_map(
        on_device,
        mesh=mesh,
        in_specs=placed,
        out_specs=(P("dp", "tm", "height", None, None), P(("tm", "height"), None, None)),
        check_vma=False,
    )
```

time: 98 us -> 86.9 us (0.89)
  the two profiles are of different devices: /device:TPU:110 before, /device:TPU:8 now
where the time goes in v2:
time: 86.9 us; the launch traced here: 85.5 us
  Pallas kernels  81.7 us (94%)
  local copies, waits for them, and re-layouts  3.2 us (4%)
    pallas_call x1, Pallas kernels, on_device(): pl.pallas_call(functools.partial(body, scale), out_shape=(jax.ShapeDtypeS...  81.7 us
    unnamed x2, local copies, waits for them, and re-layouts  3.2 us

profile of v2, /device:TPU:8, one launch (start us, length us, event | category | flops | bytes accessed | tf_op | source)
XLA Modules:
  0.0 85.5 jit_solution(10510962527628644363)
XLA Ops:
  0.6 81.7 %shard_map.77 = (bf16[2,64,512]{2,1,0:T(8,128)(2,1)}, f32[27,8,256]{2,1,0:T(8,128)}) custom-call(bf16[2,64,512]{2,1,0:T(8,128)(2,1)} %bitcast.8, bf16[2,256,256]{2,1,0:T(8,128)(2,1)} %bitcast.6, bf16[27,32,512]{2,1,0:T(8,128)(2,1)} %bitcast.5, bf16[27,512,256]{2,1,0:T(8,128)(2,1)} %w2_in.1, bf16[672,256]{1,0:T(8,128)(2,1)} %constant.4.clone.sums_in, ...), custom_call_target="tpu_custom_call" | custom-call | tf_op jit(solution)/shard_map/pallas_call | solution.py:537
  82.3 1.6 %copy.10 = bf16[1,2,4,16,512]{4,3,2,1,0:T(8,128)(2,1)} copy(bf16[1,2,4,16,512]{4,3,2,1,0:T(8,128)(2,1)} %bitcast.9) | data formatting | bytes 262144
  83.9 1.6 %copy.11 = f32[8,27,256]{2,0,1:T(8,128)} copy(f32[8,27,256]{2,0,1:T(8,128)} %bitcast.7) | data formatting | bytes 442368

commit v3 on v2

--- a/solution.py
+++ b/solution.py
@@ -44,9 +44,9 @@
     scale,
     lat_in, og_in, wt_in, w2_in, sums_in, eye_in,
     gi_out, gw_out,
-    xg, og, w, w2, g, gh, acc, q, qh, pre, ga, es, er,
+    xg, og, w, w2, g, gh, acc, ah, q, qh, pre, ga, es, er,
     act, gp3, act3, act3t, hal3t, gi, pb, rp, ps, rr, gws, ra, sbf, sb, rb, fc, rc,
-    loc_s, ag_s, ag_r, wz_s, wz_r, wx_s, wx_r, e_s, e_r, pr_s, pr_r, rs_s, rs_r,
+    loc_s, w2_s, ag_s, ag_r, wz_s, wz_r, wx_s, wx_r, e_s, e_r, pr_s, pr_r, rs_s, rs_r,
     a_s, a_r, b_s, b_r, c_s, c_r,
 ):
     x = lax.axis_index("dp")
@@ -89,9 +89,12 @@
     own_w = pltpu.make_async_copy(wt_in, w.at[:, pos % 2], loc_s.at[2])
     w2_copies = [
         pltpu.make_async_copy(
-            w2_in.at[pl.ds(9 * a, 9), pl.ds(pl.multiple_of(base, 64), 64)], w2.at[:, a], loc_s.at[3 + a]
+            w2_in.at[9 * a + k, pl.ds(pl.multiple_of(base, 64), 64)],
+            w2.at[64 * a : 64 * a + 64, 256 * k : 256 * k + 256],
+            w2_s.at[a, k],
         )
         for a in range(3)
+        for k in range(9)
     ]
 
     @pl.when(source)
@@ -122,6 +125,7 @@
     for copy in w2_copies:
         copy.start()
     acc[...] = jnp.zeros_like(acc)
+    ah[...] = jnp.zeros_like(ah)
 
     @pl.when(source)
     def _():
@@ -131,7 +135,7 @@
         copy.wait()
     pl.semaphore_wait(barrier, 14 + 3 * swaps.astype(jnp.int32))
 
-    arrays = (xg, og)
+    arrays = (og, xg)
 
     def gather(n, i):
         ref = arrays[n]
@@ -150,12 +154,13 @@
         }[i]()
         return remote(place, place, ag_s.at[n, i], ag_r.at[n, i], target)
 
-    reach = (4, 3)
+    reach = (4, 3, 3, 3)
+    cuts = (0, 16, 20, 24, 27)
 
     def share(part, slot):
         if part == 0:
             return w.at[pl.ds(4 * x, 4), slot]
-        return w.at[16:27, slot]
+        return w.at[cuts[part] : cuts[part + 1], slot]
 
     def along_z(part, slot, way):
         target = dev(x, y, up_z if way == 0 else down_z, c)
@@ -174,10 +179,10 @@
         def _():
             act_on(along_z(part, slot, 1))
 
-    def z_recv(part, slot):
-        @pl.when(pos != slot)
-        def _():
-            along_z(part, slot, 0).wait_recv()
+    def goes_on(part, slot):
+        far = (pos + NZ - slot) % NZ
+        r = reach[part]
+        return jnp.logical_and(far != 0, jnp.logical_or(far < r, far > r + 1))
 
     def along_x(slot, i):
         up, down = dev(up_x, y, z, c), dev(down_x, y, z, c)
@@ -193,8 +198,8 @@
     def start(copy):
         copy.start()
 
-    near = jnp.where(jnp.logical_and(pos >= 1, pos <= 4), 1, 0)
-    slots = (near, 1 - near)
+    closer = jnp.where(jnp.logical_and(pos >= 1, pos <= 4), 1, 0)
+    slots = (closer, 1 - closer)
     own_slot = pos % 2
 
     @pl.when(source)
@@ -207,12 +212,14 @@
     @pl.when(source)
     def _():
         z_sends(1, own_slot, start)
+        z_sends(2, own_slot, start)
+        z_sends(3, own_slot, start)
 
     for i in range(5):
         gather(1, i).start()
 
     def pass_on(part, slot):
-        @pl.when(pos != slot)
+        @pl.when(pos != slot if part == 0 else goes_on(part, slot))
         def _():
             along_z(part, slot, 0).wait_recv()
             z_sends(part, slot, start)
@@ -220,6 +227,11 @@
                 along_x(slot, 0).start()
                 along_x(slot, 1).start()
 
+    def pass_end(part, slot):
+        @pl.when(jnp.logical_and(pos != slot, jnp.logical_not(goes_on(part, slot))))
+        def _():
+            along_z(part, slot, 0).wait_recv()
+
     def pass_x(slot):
         @pl.when(pos != slot)
         def _():
@@ -245,44 +257,44 @@
         gather(n, 6).wait_recv()
         gather(n, 9).start()
 
-    pass_on(0, slots[0])
+    near, far = slots
+    pass_on(0, near)
     pass_y(0)
-    pass_on(0, slots[1])
+    pass_on(1, near)
+    pass_on(0, far)
     pass_mate(0)
-    pass_x(slots[0])
-    pass_on(1, slots[0])
+    pass_on(2, near)
+    pass_on(1, far)
+    pass_x(near)
     pass_y(1)
     pass_far(0)
-    pass_x(slots[1])
-    pass_on(1, slots[1])
+    pass_on(3, near)
+    pass_on(2, far)
     pass_mate(1)
     pass_far(1)
 
     for i in (4, 7, 8, 9):
         gather(0, i).wait_recv()
-    for slot in range(2):
-        @pl.when(pos != slot)
-        def _():
-            along_x(slot, 2).wait_recv()
-            along_x(slot, 3).wait_recv()
-
-    for a in range(3):
-        n = 6 + a
-        for b in range(3):
-            k = 9 * a + 3 * b
-            part = dot(xg[0:n].reshape(n * 128, 512), w[k : k + 3].reshape(192, 512), NT)
-            acc[2 - a : 8, :, 16 * (2 - b) : 16 * (2 - b) + 64, :] += part.reshape(n, 2, 64, 192)
-
-    col96 = lax.broadcasted_iota(jnp.int32, (192, 64), 0) % 16
-
-    def columns(t, _):
-        part = acc[t].reshape(192, 192)
-        before = jnp.where(col96 == 0, 0.0, pltpu.roll(part[:, 0:64], 1, 0))
-        after = jnp.where(col96 == 15, 0.0, pltpu.roll(part[:, 128:192], 191, 0))
-        pre[t] = (before + part[:, 64:128] + after).reshape(2, 96, 64)
+
+    def sums_of(f, band):
+        part = dot(sums_in[...], og[f, band], NN)
+        for k in range(9):
+            g[f, band, :, 256 * k : 256 * k + 256] = part[64 * k : 64 * k + 64].astype(BF)
+        for k in range(6):
+            lane = 256 * (k % 3)
+            gh[k // 3, f, band, :, lane : lane + 256] = part[576 + 16 * k : 592 + 16 * k].astype(BF)
+
+    def sum_step(f, _):
+        sums_of(f, 0)
+        sums_of(f, 1)
         return 0
 
-    lax.fori_loop(0, 8, columns, 0)
+    lax.fori_loop(0, 4, sum_step, 0)
+    pass_x(far)
+    pass_on(3, far)
+    lax.fori_loop(4, 8, sum_step, 0)
+    for copy in w2_copies:
+        copy.wait()
 
     def edge_copy(n, side):
         target = dev(x, y, down_z if side == 0 else up_z, c)
@@ -305,39 +317,6 @@
         if side == 0:
             return jnp.where(last, jnp.stack([v[1], jnp.zeros_like(v[1])]), v)
         return jnp.where(first, jnp.stack([jnp.zeros_like(v[0]), v[0]]), v)
-
-    edge_send(0, lambda side, t: pre[t, :, 80 * side : 80 * side + 16])
-
-    for i in (4, 7, 8, 9):
-        gather(1, i).wait_recv()
-
-    def sum_step(i, _):
-        f, band = i // 2, i % 2
-        part = dot(sums_in[...], og[f, band], NN)
-        for k in range(9):
-            g[k, f, band] = part[64 * k : 64 * k + 64].astype(BF)
-        for k in range(6):
-            gh[k, f, band] = part[576 + 16 * k : 592 + 16 * k].astype(BF)
-        return 0
-
-    lax.fori_loop(0, 16, sum_step, 0)
-    for copy in w2_copies:
-        copy.wait()
-    q[...] = jnp.zeros_like(q)
-
-    def q_step(k, _):
-        wk = w2[k].reshape(192, 256)
-        q[...] += dot(g[k].reshape(1024, 256), wk, NT).reshape(8, 2, 64, 192)
-        return 0
-
-    lax.fori_loop(0, 9, q_step, 0)
-    for side in range(2):
-        total = None
-        for e in range(3):
-            wk = w2[6 * side + e].reshape(192, 256)
-            term = dot(gh[3 * side + e].reshape(256, 256), wk, NT)
-            total = term if total is None else total + term
-        qh[side] = total.reshape(8, 2, 16, 192)
 
     def through_time(ref, t):
         out = ref[t, :, :, 128:192]
@@ -347,9 +326,57 @@
             out = out + ref[t + 2, :, :, 0:64]
         return out
 
+    for side in range(2):
+        lanes = slice(1536 * side, 1536 * side + 768)
+        qh[side] = dot(gh[side].reshape(256, 768), w2[:, lanes], NT).reshape(8, 2, 16, 192)
     edge_send(1, lambda side, t: through_time(qh.at[side], t))
+    q[...] = dot(g[...].reshape(1024, 2304), w2[...], NT).reshape(8, 2, 64, 192)
     for t in range(8):
         ga[t] = through_time(q, t)
+
+    for i in (4, 7, 8, 9):
+        gather(1, i).wait_recv()
+    for slot in range(2):
+        for part in range(1, 4):
+            pass_end(part, slot)
+
+        @pl.when(pos != slot)
+        def _():
+            along_x(slot, 2).wait_recv()
+            along_x(slot, 3).wait_recv()
+
+    def summed_columns(part):
+        rows = part.shape[0]
+        col = lax.broadcasted_iota(jnp.int32, (rows, 64), 0) % 16
+        before = jnp.where(col == 0, 0.0, pltpu.roll(part[:, 0:64], 1, 0))
+        after = jnp.where(col == 15, 0.0, pltpu.roll(part[:, 128:192], rows - 1, 0))
+        return before + part[:, 64:128] + after
+
+    for side in range(2):
+        for a in range(3):
+            n = 6 + a
+            k = 9 * a + 6 * (1 - side)
+            rows = xg[0:n, :, 48 * side : 48 * side + 16].reshape(n * 32, 512)
+            part = dot(rows, w[k : k + 3].reshape(192, 512), NT)
+            ah[side, 2 - a : 8] += part.reshape(n, 2, 16, 192)
+    edge_send(0, lambda side, t: summed_columns(ah[side, t].reshape(32, 192)).reshape(2, 16, 64))
+
+    for a in range(3):
+        n = 6 + a
+        for b in range(3):
+            k = 9 * a + 3 * b
+            lo = 16 if b == 2 else 0
+            to = 16 if b == 0 else 0
+            size = 64 if b == 1 else 48
+            rows = xg[0:n, :, lo : lo + size].reshape(n * 2 * size, 512)
+            part = dot(rows, w[k : k + 3].reshape(192, 512), NT)
+            acc[2 - a : 8, :, to : to + size, :] += part.reshape(n, 2, size, 192)
+
+    def columns(t, _):
+        pre[t, :, 16:80] = summed_columns(acc[t].reshape(128, 192)).reshape(2, 64, 64)
+        return 0
+
+    lax.fori_loop(0, 8, columns, 0)
 
     edge_wait(0)
     for t in range(8):
@@ -387,25 +414,34 @@
         ).astype(BF)
         hal3t[side] = dot(eye_in[...], stack, NT).astype(BF)
 
-    for k in range(9):
-        part = dot(act3t[...], g[k].reshape(1024, 256), NN)
-        if k // 3 != 1:
-            side = k // 6
-            part = part + dot(hal3t[side], gh[3 * side + k % 3].reshape(256, 256), NN)
-        gws[3 * k : 3 * k + 3] = part.astype(BF).reshape(3, 64, 256)
+    for b in range(3):
+        part = dot(act3t[...], g[:, :, :, 768 * b : 768 * b + 768].reshape(1024, 768), NN)
+        if b != 1:
+            part = part + dot(hal3t[b // 2], gh[b // 2].reshape(256, 768), NN)
+        for e in range(3):
+            k = 3 * b + e
+            gws[3 * k : 3 * k + 3] = part[:, 256 * e : 256 * e + 256].astype(BF).reshape(3, 64, 256)
     gws[27] = jnp.zeros((64, 256), BF)
 
-    def x_copy(d):
+    size, place = (4, 3), (0, 4)
+
+    def x_copy(d, i):
         to = (x + d) % 4
-        return remote(gws.at[pl.ds(7 * to, 7)], ra.at[d - 1], a_s.at[d - 1], a_r.at[d - 1], dev(to, y, z, c))
-
-    for d in (2, 1, 3):
-        x_copy(d).start()
+        return remote(
+            gws.at[pl.ds(7 * to + place[i], size[i])], ra.at[d - 1, place[i] : place[i] + size[i]],
+            a_s.at[d - 1, i], a_r.at[d - 1, i], dev(to, y, z, c),
+        )
+
+    for i in range(2):
+        for d in (2, 1, 3):
+            x_copy(d, i).start()
 
     edge_wait(3)
     for t in range(8):
         pre[t, :, 0:16] = edge_rows(3, 1, t)
         pre[t, :, 80:96] = edge_rows(3, 0, t)
+
+    col96 = lax.broadcasted_iota(jnp.int32, (192, 64), 0) % 16
 
     def shifted(t, _):
         part = pre[t].reshape(192, 64)
@@ -430,27 +466,35 @@
     pair_copy = remote(pb, rp, pr_s, pr_r, dev(x, y, z, 1 - c))
     pair_copy.start()
 
-    for d in range(1, 4):
-        x_copy(d).wait_recv()
-
-    def x_sum(j, _):
-        total = gws[7 * x + j].astype(F32)
-        for d in range(3):
-            total = total + ra[d, j].astype(F32)
-        sbf[:, pl.ds(pl.multiple_of(8 * j, 8), 8)] = total.reshape(8, 8, 256)
-        return 0
-
-    lax.fori_loop(0, 7, x_sum, 0)
     sbf[:, 56:64] = jnp.zeros((8, 8, 256), F32)
-    sb[...] = sbf[...].astype(BF)
-
-    def z_copy(d):
+
+    def z_copy(d, i):
         to = (z + d) % NZ
-        return remote(sb.at[to], rb.at[d - 1], b_s.at[d - 1], b_r.at[d - 1], dev(x, y, to, c))
-
-    for d in (4, 3, 5, 2, 6, 1, 7):
-        z_copy(d).start()
-
+        half = slice(32 * i, 32 * i + 32)
+        return remote(sb.at[to, half], rb.at[d - 1, half], b_s.at[d - 1, i], b_r.at[d - 1, i], dev(x, y, to, c))
+
+    def x_sum(i):
+        for d in range(1, 4):
+            x_copy(d, i).wait_recv()
+        for j in range(place[i], place[i] + size[i]):
+            total = gws[7 * x + j].astype(F32)
+            for d in range(3):
+                total = total + ra[d, j].astype(F32)
+            sbf[:, 8 * j : 8 * j + 8] = total.reshape(8, 8, 256)
+        sb[:, 32 * i : 32 * i + 32] = sbf[:, 32 * i : 32 * i + 32].astype(BF)
+        for d in (4, 3, 5, 2, 6, 1, 7):
+            z_copy(d, i).start()
+
+    def z_sum(i):
+        half = slice(32 * i, 32 * i + 32)
+        for d in range(1, NZ):
+            z_copy(d, i).wait_recv()
+        total = sb[z, half].astype(F32)
+        for d in range(NZ - 1):
+            total = total + rb[d, half].astype(F32)
+        fc[half] = (total * scale).astype(BF)
+
+    x_sum(0)
     pair_copy.wait_recv()
     for half in range(2):
         for f in range(2):
@@ -463,12 +507,9 @@
     for d in (2, 1, 3):
         y_copy(d).start()
 
-    for d in range(1, NZ):
-        z_copy(d).wait_recv()
-    total = sb[z].astype(F32)
-    for d in range(NZ - 1):
-        total = total + rb[d].astype(F32)
-    fc[...] = (total * scale).astype(BF)
+    x_sum(1)
+    z_sum(0)
+    z_sum(1)
 
     def out_copy(to_x):
         return remote(fc, rc.at[x], c_s.at[to_x], c_r.at[x], dev(to_x, y_out, z, c))
@@ -505,8 +546,9 @@
     for n in range(2):
         for i in range(10):
             gather(n, i).wait_send()
+    for part in range(4):
         for slot in range(2):
-            z_sends(n, slot, sent)
+            z_sends(part, slot, sent)
     for slot in range(2):
         @pl.when(pos != slot)
         def _():
@@ -518,10 +560,12 @@
             edge_copy(n, side).wait_send()
     pair_copy.wait_send()
     for d in range(1, 4):
-        x_copy(d).wait_send()
+        x_copy(d, 0).wait_send()
+        x_copy(d, 1).wait_send()
         y_copy(d).wait_send()
     for d in range(1, NZ):
-        z_copy(d).wait_send()
+        z_copy(d, 0).wait_send()
+        z_copy(d, 1).wait_send()
     for to_x in range(4):
         @pl.when(jnp.logical_not(jnp.logical_and(x == to_x, y == y_out)))
         def _():
@@ -546,10 +590,11 @@
             pltpu.VMEM((8, 2, 64, 512), BF),
             pltpu.VMEM((8, 2, 256, 256), BF),
             pltpu.VMEM((27, 2, 32, 512), BF),
-            pltpu.VMEM((9, 3, 64, 256), BF),
-            pltpu.VMEM((9, 8, 2, 64, 256), BF),
-            pltpu.VMEM((6, 8, 2, 16, 256), BF),
-            pltpu.VMEM((8, 2, 96, 192), F32),
+            pltpu.VMEM((192, 2304), BF),
+            pltpu.VMEM((8, 2, 64, 2304), BF),
+            pltpu.VMEM((2, 8, 2, 16, 768), BF),
+            pltpu.VMEM((8, 2, 64, 192), F32),
+            pltpu.VMEM((2, 8, 2, 16, 192), F32),
             pltpu.VMEM((8, 2, 64, 192), F32),
             pltpu.VMEM((2, 8, 2, 16, 192), F32),
             pltpu.VMEM((8, 2, 96, 64), F32),
@@ -573,15 +618,15 @@
             pltpu.VMEM((7, 64, 256), BF),
             pltpu.VMEM((64, 256), BF),
             pltpu.VMEM((4, 64, 256), BF),
-            dma((6,)),
+            dma((3,)), dma((3, 9)),
             dma((2, 10)), dma((2, 10)),
-            dma((2, 2, 2)), dma((2, 2)),
+            dma((4, 2, 2)), dma((4, 2)),
             dma((2, 4)), dma((2, 4)),
             dma((4, 2)), dma((4, 2)),
             dma, dma,
             dma((3,)), dma((3,)),
-            dma((3,)), dma((3,)),
-            dma((7,)), dma((7,)),
+            dma((3, 2)), dma((3, 2)),
+            dma((7, 2)), dma((7, 2)),
             dma((4,)), dma((4,)),
         ],
         compiler_params=pltpu.CompilerParams(

time: 86.9 us -> 78.5 us (0.903); the launches traced: 85.5 us -> 78.1 us
  Pallas kernels: 81.7 us -> 74.3 us
    pallas_call x1, Pallas kernels: 81.7 us -> 74.3 us  [on_device(): pl.pallas_call(functools.partial(body, scale), out_shape=(jax.ShapeDtypeS...]
where the time goes in v3:
time: 78.5 us; the launch traced here: 78.1 us
  Pallas kernels  74.3 us (95%)
  local copies, waits for them, and re-layouts  3.2 us (4%)
    pallas_call x1, Pallas kernels, on_device(): pl.pallas_call(functools.partial(body, scale), out_shape=(jax.ShapeDtypeS...  74.3 us
    unnamed x2, local copies, waits for them, and re-layouts  3.2 us

profile of v3, /device:TPU:8, one launch (start us, length us, event | category | flops | bytes accessed | tf_op | source)
XLA Modules:
  0.0 78.1 jit_solution(15995461899844382944)
XLA Ops:
  0.6 74.3 %shard_map.77 = (bf16[2,64,512]{2,1,0:T(8,128)(2,1)}, f32[27,8,256]{2,1,0:T(8,128)}) custom-call(bf16[2,64,512]{2,1,0:T(8,128)(2,1)} %bitcast.8, bf16[2,256,256]{2,1,0:T(8,128)(2,1)} %bitcast.6, bf16[27,32,512]{2,1,0:T(8,128)(2,1)} %bitcast.5, bf16[27,512,256]{2,1,0:T(8,128)(2,1)} %w2_in.1, bf16[672,256]{1,0:T(8,128)(2,1)} %constant.4.clone.sums_in, ...), custom_call_target="tpu_custom_call" | custom-call | tf_op jit(solution)/shard_map/pallas_call | solution.py:581
  74.9 1.6 %copy.10 = bf16[1,2,4,16,512]{4,3,2,1,0:T(8,128)(2,1)} copy(bf16[1,2,4,16,512]{4,3,2,1,0:T(8,128)(2,1)} %bitcast.9) | data formatting | bytes 262144
  76.5 1.6 %copy.11 = f32[8,27,256]{2,0,1:T(8,128)} copy(f32[8,27,256]{2,0,1:T(8,128)} %bitcast.7) | data formatting | bytes 442368

commit v4 on v3

--- a/solution.py
+++ b/solution.py
@@ -36,6 +36,15 @@
     return np.concatenate([main.reshape(576, 256), edge.reshape(96, 256)], axis=0)
 
 
+def tap_places():
+    middle = [(1, e, a) for e in range(3) for a in range(3)]
+    rest = [middle[8]] + [(b, e, a) for b in (0, 2) for e in range(3) for a in range(3)]
+    places = []
+    for x in range(4):
+        places += middle[2 * x : 2 * x + 2] + rest[5 * x : 5 * x + 5]
+    return places
+
+
 def dot(a, b, dims):
     return lax.dot_general(a, b, dims, preferred_element_type=F32)
 
@@ -45,7 +54,7 @@
     lat_in, og_in, wt_in, w2_in, sums_in, eye_in,
     gi_out, gw_out,
     xg, og, w, w2, g, gh, acc, ah, q, qh, pre, ga, es, er,
-    act, gp3, act3, act3t, hal3t, gi, pb, rp, ps, rr, gws, ra, sbf, sb, rb, fc, rc,
+    act, gp3, act3, act3t, gi, pb, rp, ps, rr, gws, ra, sbf, sb, rb, fc, rc,
     loc_s, w2_s, ag_s, ag_r, wz_s, wz_r, wx_s, wx_r, e_s, e_r, pr_s, pr_r, rs_s, rs_r,
     a_s, a_r, b_s, b_r, c_s, c_r,
 ):
@@ -154,13 +163,13 @@
         }[i]()
         return remote(place, place, ag_s.at[n, i], ag_r.at[n, i], target)
 
-    reach = (4, 3, 3, 3)
-    cuts = (0, 16, 20, 24, 27)
+    reach = (4, 4, 3, 3, 3)
+    cuts = (16, 20, 24, 27)
 
     def share(part, slot):
-        if part == 0:
-            return w.at[pl.ds(4 * x, 4), slot]
-        return w.at[cuts[part] : cuts[part + 1], slot]
+        if part < 2:
+            return w.at[pl.ds(4 * x + 2 * part, 2), slot]
+        return w.at[cuts[part - 2] : cuts[part - 1], slot]
 
     def along_z(part, slot, way):
         target = dev(x, y, up_z if way == 0 else down_z, c)
@@ -186,13 +195,11 @@
 
     def along_x(slot, i):
         up, down = dev(up_x, y, z, c), dev(down_x, y, z, c)
-        first, target = {
-            0: lambda: (4 * x, up),
-            1: lambda: (4 * x, down),
-            2: lambda: (4 * down_x, up),
-            3: lambda: (4 * up_x + 2, down),
-        }[i]()
-        place = w.at[pl.ds(first, 4 if i < 2 else 2), slot]
+        first, target = (
+            (4 * x, up), (4 * x + 2, up), (4 * x + 2, down), (4 * x, down),
+            (4 * down_x, up), (4 * up_x + 2, down),
+        )[i]
+        place = w.at[pl.ds(first, 2), slot]
         return remote(place, place, wx_s.at[slot, i], wx_r.at[slot, i], target)
 
     def start(copy):
@@ -205,27 +212,28 @@
     @pl.when(source)
     def _():
         z_sends(0, own_slot, start)
+        z_sends(1, own_slot, start)
 
     for i in range(5):
         gather(0, i).start()
 
     @pl.when(source)
     def _():
-        z_sends(1, own_slot, start)
         z_sends(2, own_slot, start)
         z_sends(3, own_slot, start)
+        z_sends(4, own_slot, start)
 
     for i in range(5):
         gather(1, i).start()
 
     def pass_on(part, slot):
-        @pl.when(pos != slot if part == 0 else goes_on(part, slot))
+        @pl.when(pos != slot if part < 2 else goes_on(part, slot))
         def _():
             along_z(part, slot, 0).wait_recv()
             z_sends(part, slot, start)
-            if part == 0:
-                along_x(slot, 0).start()
-                along_x(slot, 1).start()
+            if part < 2:
+                along_x(slot, part).start()
+                along_x(slot, 3 - part).start()
 
     def pass_end(part, slot):
         @pl.when(jnp.logical_and(pos != slot, jnp.logical_not(goes_on(part, slot))))
@@ -236,9 +244,9 @@
         @pl.when(pos != slot)
         def _():
             along_x(slot, 0).wait_recv()
-            along_x(slot, 2).start()
-            along_x(slot, 1).wait_recv()
-            along_x(slot, 3).start()
+            along_x(slot, 4).start()
+            along_x(slot, 2).wait_recv()
+            along_x(slot, 5).start()
 
     def pass_y(n):
         gather(n, 0).wait_recv()
@@ -258,20 +266,41 @@
         gather(n, 9).start()
 
     near, far = slots
-    pass_on(0, near)
-    pass_y(0)
-    pass_on(1, near)
-    pass_on(0, far)
-    pass_mate(0)
-    pass_on(2, near)
-    pass_on(1, far)
-    pass_x(near)
-    pass_y(1)
-    pass_far(0)
-    pass_on(3, near)
-    pass_on(2, far)
-    pass_mate(1)
-    pass_far(1)
+    close = jnp.logical_or(pos < 3, pos == 7)
+
+    def pass_z(*steps):
+        for part, slot in steps:
+            pass_on(part, slot)
+
+    @pl.when(close)
+    def _():
+        pass_z((0, near), (1, near))
+        pass_y(0)
+        pass_z((0, far), (1, far), (2, near))
+        pass_mate(0)
+        pass_x(near)
+        pass_z((2, far), (3, near))
+        pass_y(1)
+        pass_far(0)
+        pass_x(far)
+        pass_z((3, far), (4, near))
+        pass_mate(1)
+        pass_z((4, far))
+        pass_far(1)
+
+    @pl.when(jnp.logical_not(close))
+    def _():
+        pass_y(0)
+        pass_z((0, near), (1, near))
+        pass_mate(0)
+        pass_z((0, far), (1, far))
+        pass_y(1)
+        pass_far(0)
+        pass_z((2, near))
+        pass_x(near)
+        pass_mate(1)
+        pass_z((2, far), (3, near))
+        pass_far(1)
 
     for i in (4, 7, 8, 9):
         gather(0, i).wait_recv()
@@ -290,8 +319,12 @@
         return 0
 
     lax.fori_loop(0, 4, sum_step, 0)
-    pass_x(far)
-    pass_on(3, far)
+
+    @pl.when(jnp.logical_not(close))
+    def _():
+        pass_x(far)
+        pass_z((3, far), (4, near), (4, far))
+
     lax.fori_loop(4, 8, sum_step, 0)
     for copy in w2_copies:
         copy.wait()
@@ -337,13 +370,13 @@
     for i in (4, 7, 8, 9):
         gather(1, i).wait_recv()
     for slot in range(2):
-        for part in range(1, 4):
+        for part in range(2, 5):
             pass_end(part, slot)
 
         @pl.when(pos != slot)
         def _():
-            along_x(slot, 2).wait_recv()
-            along_x(slot, 3).wait_recv()
+            for i in (1, 3, 4, 5):
+                along_x(slot, i).wait_recv()
 
     def summed_columns(part):
         rows = part.shape[0]
@@ -397,6 +430,29 @@
         act3[t] = stacked(lambda u: act[u], t).astype(BF)
     act3t[...] = dot(eye_in[...], act3[...].reshape(1024, 192), NT).astype(BF)
 
+    first_place, size = (0, 2, 6), (2, 4, 1)
+    places = tap_places()
+
+    def x_copy(d, i):
+        to = (x + d) % 4
+        lo = first_place[i]
+        return remote(
+            gws.at[pl.ds(7 * to + lo, size[i])], ra.at[d - 1, lo : lo + size[i]],
+            a_s.at[d - 1, i], a_r.at[d - 1, i], dev(to, y, z, c),
+        )
+
+    def keep(b, part):
+        for e in range(3):
+            for a in range(3):
+                gws[places.index((b, e, a))] = part[64 * a : 64 * a + 64, 256 * e : 256 * e + 256].astype(BF)
+
+    def own_cells(b):
+        return dot(act3t[...], g[:, :, :, 768 * b : 768 * b + 768].reshape(1024, 768), NN)
+
+    keep(1, own_cells(1))
+    for d in (2, 1, 3):
+        x_copy(d, 0).start()
+
     edge_wait(1)
     for t in range(8):
         ga[t, :, 0:16] += edge_rows(1, 1, t)
@@ -404,6 +460,7 @@
         pre[t, :, 16:80] = ga[t] * pre[t, :, 16:80]
     edge_send(3, lambda side, t: pre[t, :, 16 + 48 * side : 32 + 48 * side])
 
+    parts = (own_cells(0), own_cells(2))
     edge_wait(2)
     for t in range(8):
         for side in range(2):
@@ -412,27 +469,10 @@
         stack = jnp.concatenate(
             [stacked(lambda u: qh[side, u, :, :, 0:64], t).reshape(32, 192) for t in range(8)], axis=0
         ).astype(BF)
-        hal3t[side] = dot(eye_in[...], stack, NT).astype(BF)
-
-    for b in range(3):
-        part = dot(act3t[...], g[:, :, :, 768 * b : 768 * b + 768].reshape(1024, 768), NN)
-        if b != 1:
-            part = part + dot(hal3t[b // 2], gh[b // 2].reshape(256, 768), NN)
-        for e in range(3):
-            k = 3 * b + e
-            gws[3 * k : 3 * k + 3] = part[:, 256 * e : 256 * e + 256].astype(BF).reshape(3, 64, 256)
+        hal3t = dot(eye_in[...], stack, NT).astype(BF)
+        keep(2 * side, parts[side] + dot(hal3t, gh[side].reshape(256, 768), NN))
     gws[27] = jnp.zeros((64, 256), BF)
-
-    size, place = (4, 3), (0, 4)
-
-    def x_copy(d, i):
-        to = (x + d) % 4
-        return remote(
-            gws.at[pl.ds(7 * to + place[i], size[i])], ra.at[d - 1, place[i] : place[i] + size[i]],
-            a_s.at[d - 1, i], a_r.at[d - 1, i], dev(to, y, z, c),
-        )
-
-    for i in range(2):
+    for i in (1, 2):
         for d in (2, 1, 3):
             x_copy(d, i).start()
 
@@ -468,31 +508,35 @@
 
     sbf[:, 56:64] = jnp.zeros((8, 8, 256), F32)
 
+    def rows_of(i):
+        return slice(8 * first_place[i], 8 * first_place[i] + max(8 * size[i], 16))
+
     def z_copy(d, i):
         to = (z + d) % NZ
-        half = slice(32 * i, 32 * i + 32)
-        return remote(sb.at[to, half], rb.at[d - 1, half], b_s.at[d - 1, i], b_r.at[d - 1, i], dev(x, y, to, c))
+        part = rows_of(i)
+        return remote(sb.at[to, part], rb.at[d - 1, part], b_s.at[d - 1, i], b_r.at[d - 1, i], dev(x, y, to, c))
 
     def x_sum(i):
         for d in range(1, 4):
             x_copy(d, i).wait_recv()
-        for j in range(place[i], place[i] + size[i]):
+        for j in range(first_place[i], first_place[i] + size[i]):
             total = gws[7 * x + j].astype(F32)
             for d in range(3):
                 total = total + ra[d, j].astype(F32)
             sbf[:, 8 * j : 8 * j + 8] = total.reshape(8, 8, 256)
-        sb[:, 32 * i : 32 * i + 32] = sbf[:, 32 * i : 32 * i + 32].astype(BF)
+        part = rows_of(i)
+        sb[:, part] = sbf[:, part].astype(BF)
         for d in (4, 3, 5, 2, 6, 1, 7):
             z_copy(d, i).start()
 
     def z_sum(i):
-        half = slice(32 * i, 32 * i + 32)
+        part = rows_of(i)
         for d in range(1, NZ):
             z_copy(d, i).wait_recv()
-        total = sb[z, half].astype(F32)
+        total = sb[z, part].astype(F32)
         for d in range(NZ - 1):
-            total = total + rb[d, half].astype(F32)
-        fc[half] = (total * scale).astype(BF)
+            total = total + rb[d, part].astype(F32)
+        fc[part] = (total * scale).astype(BF)
 
     x_sum(0)
     pair_copy.wait_recv()
@@ -509,7 +553,9 @@
 
     x_sum(1)
     z_sum(0)
+    x_sum(2)
     z_sum(1)
+    z_sum(2)
 
     def out_copy(to_x):
         return remote(fc, rc.at[x], c_s.at[to_x], c_r.at[x], dev(to_x, y_out, z, c))
@@ -536,9 +582,9 @@
         pltpu.make_async_copy(fc, rc.at[part], c_r.at[part]).wait()
         v = rc[part].astype(F32)
         for j in range(7):
-            k, a = (7 * part + j) // 3, (7 * part + j) % 3
-            if k < 9:
-                gw_out[9 * a + k] = v[8 * j : 8 * j + 8]
+            if 7 * part + j < 27:
+                b, e, a = places[7 * part + j]
+                gw_out[9 * a + 3 * b + e] = v[8 * j : 8 * j + 8]
 
     def sent(copy):
         copy.wait_send()
@@ -546,13 +592,13 @@
     for n in range(2):
         for i in range(10):
             gather(n, i).wait_send()
-    for part in range(4):
+    for part in range(5):
         for slot in range(2):
             z_sends(part, slot, sent)
     for slot in range(2):
         @pl.when(pos != slot)
         def _():
-            for i in range(4):
+            for i in range(6):
                 along_x(slot, i).wait_send()
 
     for n in range(4):
@@ -560,12 +606,12 @@
             edge_copy(n, side).wait_send()
     pair_copy.wait_send()
     for d in range(1, 4):
-        x_copy(d, 0).wait_send()
-        x_copy(d, 1).wait_send()
+        for i in range(3):
+            x_copy(d, i).wait_send()
         y_copy(d).wait_send()
     for d in range(1, NZ):
-        z_copy(d, 0).wait_send()
-        z_copy(d, 1).wait_send()
+        for i in range(3):
+            z_copy(d, i).wait_send()
     for to_x in range(4):
         @pl.when(jnp.logical_not(jnp.logical_and(x == to_x, y == y_out)))
         def _():
@@ -605,7 +651,6 @@
             pltpu.VMEM((8, 2, 96, 192), BF),
             pltpu.VMEM((8, 2, 64, 192), BF),
             pltpu.VMEM((192, 1024), BF),
-            pltpu.VMEM((2, 192, 256), BF),
             pltpu.VMEM((8, 2, 64, 512), F32),
             pltpu.VMEM((2, 2, 2, 64, 512), BF),
             pltpu.VMEM((2, 2, 2, 64, 512), BF),
@@ -620,13 +665,13 @@
             pltpu.VMEM((4, 64, 256), BF),
             dma((3,)), dma((3, 9)),
             dma((2, 10)), dma((2, 10)),
-            dma((4, 2, 2)), dma((4, 2)),
-            dma((2, 4)), dma((2, 4)),
+            dma((5, 2, 2)), dma((5, 2)),
+            dma((2, 6)), dma((2, 6)),
             dma((4, 2)), dma((4, 2)),
             dma, dma,
             dma((3,)), dma((3,)),
-            dma((3, 2)), dma((3, 2)),
-            dma((7, 2)), dma((7, 2)),
+            dma((3, 3)), dma((3, 3)),
+            dma((7, 3)), dma((7, 3)),
             dma((4,)), dma((4,)),
         ],
         compiler_params=pltpu.CompilerParams(

time: 78.5 us -> 75 us (0.955)
  Pallas kernels: 74.3 us -> 71 us
    pallas_call x1, Pallas kernels: 74.3 us -> 71 us  [on_device(): pl.pallas_call(functools.partial(body, scale), out_shape=(jax.ShapeDtypeS...]
where the time goes in v4:
time: 75 us; the launch traced here: 74.8 us
  Pallas kernels  71 us (95%)
  local copies, waits for them, and re-layouts  3.2 us (4%)
    pallas_call x1, Pallas kernels, on_device(): pl.pallas_call(functools.partial(body, scale), out_shape=(jax.ShapeDtypeS...  71 us
    unnamed x2, local copies, waits for them, and re-layouts  3.2 us

profile of v4, /device:TPU:8, one launch (start us, length us, event | category | flops | bytes accessed | tf_op | source)
XLA Modules:
  0.0 74.8 jit_solution(5050562989721844078)
XLA Ops:
  0.6 71.0 %shard_map.77 = (bf16[2,64,512]{2,1,0:T(8,128)(2,1)}, f32[27,8,256]{2,1,0:T(8,128)}) custom-call(bf16[2,64,512]{2,1,0:T(8,128)(2,1)} %bitcast.8, bf16[2,256,256]{2,1,0:T(8,128)(2,1)} %bitcast.6, bf16[27,32,512]{2,1,0:T(8,128)(2,1)} %bitcast.5, bf16[27,512,256]{2,1,0:T(8,128)(2,1)} %w2_in.1, bf16[672,256]{1,0:T(8,128)(2,1)} %constant.4.clone.sums_in, ...), custom_call_target="tpu_custom_call" | custom-call | tf_op jit(solution)/shard_map/pallas_call | solution.py:627
  71.6 1.6 %copy.10 = bf16[1,2,4,16,512]{4,3,2,1,0:T(8,128)(2,1)} copy(bf16[1,2,4,16,512]{4,3,2,1,0:T(8,128)(2,1)} %bitcast.9) | data formatting | bytes 262144
  73.2 1.6 %copy.11 = f32[8,27,256]{2,0,1:T(8,128)} copy(f32[8,27,256]{2,0,1:T(8,128)} %bitcast.7) | data formatting | bytes 442368

commit v5 on v4

--- a/solution.py
+++ b/solution.py
@@ -163,21 +163,36 @@
         }[i]()
         return remote(place, place, ag_s.at[n, i], ag_r.at[n, i], target)
 
-    reach = (4, 4, 3, 3, 3)
-    cuts = (16, 20, 24, 27)
+    reach = (4, 4, 3)
 
     def share(part, slot):
         if part < 2:
-            return w.at[pl.ds(4 * x + 2 * part, 2), slot]
-        return w.at[cuts[part - 2] : cuts[part - 1], slot]
+            return w.at[pl.ds(6 * x + 3 * part, 3), slot]
+        return w.at[24:27, slot]
 
     def along_z(part, slot, way):
-        target = dev(x, y, up_z if way == 0 else down_z, c)
+        step = (1, NZ - 1, 2, NZ - 2)[way]
+        target = dev(x, y, (z + step) % NZ, c)
         place = share(part, slot)
         return remote(place, place, wz_s.at[part, slot, way], wz_r.at[part, slot], target)
 
     def z_sends(part, slot, act_on):
         far = (pos + NZ - slot) % NZ
+        if part < 2:
+            @pl.when(far < 3)
+            def _():
+                act_on(along_z(part, slot, 2))
+
+            @pl.when(far == 0)
+            def _():
+                act_on(along_z(part, slot, 0))
+                act_on(along_z(part, slot, 1))
+
+            @pl.when(jnp.logical_or(far == 0, far == NZ - 1))
+            def _():
+                act_on(along_z(part, slot, 3))
+
+            return
         r = reach[part]
 
         @pl.when(far < r)
@@ -196,10 +211,10 @@
     def along_x(slot, i):
         up, down = dev(up_x, y, z, c), dev(down_x, y, z, c)
         first, target = (
-            (4 * x, up), (4 * x + 2, up), (4 * x + 2, down), (4 * x, down),
-            (4 * down_x, up), (4 * up_x + 2, down),
+            (6 * x, up), (6 * x + 3, up), (6 * x + 3, down), (6 * x, down),
+            (6 * down_x, up), (6 * up_x + 3, down),
         )[i]
-        place = w.at[pl.ds(first, 2), slot]
+        place = w.at[pl.ds(first, 3), slot]
         return remote(place, place, wx_s.at[slot, i], wx_r.at[slot, i], target)
 
     def start(copy):
@@ -220,8 +235,6 @@
     @pl.when(source)
     def _():
         z_sends(2, own_slot, start)
-        z_sends(3, own_slot, start)
-        z_sends(4, own_slot, start)
 
     for i in range(5):
         gather(1, i).start()
@@ -272,20 +285,37 @@
         for part, slot in steps:
             pass_on(part, slot)
 
+    def sums_of(f, band):
+        part = dot(sums_in[...], og[f, band], NN)
+        for k in range(9):
+            g[f, band, :, 256 * k : 256 * k + 256] = part[64 * k : 64 * k + 64].astype(BF)
+        for k in range(6):
+            lane = 256 * (k % 3)
+            gh[k // 3, f, band, :, lane : lane + 256] = part[576 + 16 * k : 592 + 16 * k].astype(BF)
+
+    def sums(core, half):
+        def step(f, _):
+            sums_of(4 * half + 2 * core + f, 0)
+            sums_of(4 * half + 2 * core + f, 1)
+            return 0
+
+        lax.fori_loop(0, 2, step, 0)
+
     @pl.when(close)
     def _():
         pass_z((0, near), (1, near))
         pass_y(0)
-        pass_z((0, far), (1, far), (2, near))
+        pass_z((0, far), (1, far))
+        pass_z((2, near))
         pass_mate(0)
         pass_x(near)
-        pass_z((2, far), (3, near))
+        pass_z((2, far))
         pass_y(1)
         pass_far(0)
         pass_x(far)
-        pass_z((3, far), (4, near))
+        sums(c, 0)
         pass_mate(1)
-        pass_z((4, far))
+        sums(c, 1)
         pass_far(1)
 
     @pl.when(jnp.logical_not(close))
@@ -296,36 +326,20 @@
         pass_z((0, far), (1, far))
         pass_y(1)
         pass_far(0)
+        pass_x(near)
         pass_z((2, near))
-        pass_x(near)
         pass_mate(1)
-        pass_z((2, far), (3, near))
+        sums(c, 0)
+        pass_x(far)
+        pass_z((2, far))
         pass_far(1)
+        sums(c, 1)
 
     for i in (4, 7, 8, 9):
         gather(0, i).wait_recv()
-
-    def sums_of(f, band):
-        part = dot(sums_in[...], og[f, band], NN)
-        for k in range(9):
-            g[f, band, :, 256 * k : 256 * k + 256] = part[64 * k : 64 * k + 64].astype(BF)
-        for k in range(6):
-            lane = 256 * (k % 3)
-            gh[k // 3, f, band, :, lane : lane + 256] = part[576 + 16 * k : 592 + 16 * k].astype(BF)
-
-    def sum_step(f, _):
-        sums_of(f, 0)
-        sums_of(f, 1)
-        return 0
-
-    lax.fori_loop(0, 4, sum_step, 0)
-
-    @pl.when(jnp.logical_not(close))
-    def _():
-        pass_x(far)
-        pass_z((3, far), (4, near), (4, far))
-
-    lax.fori_loop(4, 8, sum_step, 0)
+    sums(1 - c, 0)
+
+    sums(1 - c, 1)
     for copy in w2_copies:
         copy.wait()
 
@@ -370,8 +384,7 @@
     for i in (4, 7, 8, 9):
         gather(1, i).wait_recv()
     for slot in range(2):
-        for part in range(2, 5):
-            pass_end(part, slot)
+        pass_end(2, slot)
 
         @pl.when(pos != slot)
         def _():
@@ -592,7 +605,7 @@
     for n in range(2):
         for i in range(10):
             gather(n, i).wait_send()
-    for part in range(5):
+    for part in range(3):
         for slot in range(2):
             z_sends(part, slot, sent)
     for slot in range(2):
@@ -665,7 +678,7 @@
             pltpu.VMEM((4, 64, 256), BF),
             dma((3,)), dma((3, 9)),
             dma((2, 10)), dma((2, 10)),
-            dma((5, 2, 2)), dma((5, 2)),
+            dma((3, 2, 4)), dma((3, 2)),
             dma((2, 6)), dma((2, 6)),
             dma((4, 2)), dma((4, 2)),
             dma, dma,

time: 75 us -> 69.1 us (0.921)
  Pallas kernels: 71 us -> 65 us
    pallas_call x1, Pallas kernels: 71 us -> 65 us  [on_device(): pl.pallas_call(functools.partial(body, scale), out_shape=(jax.ShapeDtypeS...]
where the time goes in v5:
time: 69.1 us; the launch traced here: 68.9 us
  Pallas kernels  65 us (94%)
  local copies, waits for them, and re-layouts  3.2 us (5%)
    pallas_call x1, Pallas kernels, on_device(): pl.pallas_call(functools.partial(body, scale), out_shape=(jax.ShapeDtypeS...  65 us
    unnamed x2, local copies, waits for them, and re-layouts  3.2 us

profile of v5, /device:TPU:8, one launch (start us, length us, event | category | flops | bytes accessed | tf_op | source)
XLA Modules:
  0.0 68.9 jit_solution(7795018255428522682)
XLA Ops:
  0.6 65.0 %shard_map.77 = (bf16[2,64,512]{2,1,0:T(8,128)(2,1)}, f32[27,8,256]{2,1,0:T(8,128)}) custom-call(bf16[2,64,512]{2,1,0:T(8,128)(2,1)} %bitcast.8, bf16[2,256,256]{2,1,0:T(8,128)(2,1)} %bitcast.6, bf16[27,32,512]{2,1,0:T(8,128)(2,1)} %bitcast.5, bf16[27,512,256]{2,1,0:T(8,128)(2,1)} %w2_in.1, bf16[672,256]{1,0:T(8,128)(2,1)} %constant.4.clone.sums_in, ...), custom_call_target="tpu_custom_call" | custom-call | tf_op jit(solution)/shard_map/pallas_call | solution.py:640
  65.7 1.6 %copy.10 = bf16[1,2,4,16,512]{4,3,2,1,0:T(8,128)(2,1)} copy(bf16[1,2,4,16,512]{4,3,2,1,0:T(8,128)(2,1)} %bitcast.9) | data formatting | bytes 262144
  67.2 1.6 %copy.11 = f32[8,27,256]{2,0,1:T(8,128)} copy(f32[8,27,256]{2,0,1:T(8,128)} %bitcast.7) | data formatting | bytes 442368

commit v6 on v5

--- a/solution.py
+++ b/solution.py
@@ -39,10 +39,10 @@
 def tap_places():
     middle = [(1, e, a) for e in range(3) for a in range(3)]
     rest = [middle[8]] + [(b, e, a) for b in (0, 2) for e in range(3) for a in range(3)]
-    places = []
+    over_x = []
     for x in range(4):
-        places += middle[2 * x : 2 * x + 2] + rest[5 * x : 5 * x + 5]
-    return places
+        over_x += middle[2 * x : 2 * x + 2] + rest[3 * x : 3 * x + 3]
+    return over_x, rest[12:]
 
 
 def dot(a, b, dims):
@@ -54,9 +54,9 @@
     lat_in, og_in, wt_in, w2_in, sums_in, eye_in,
     gi_out, gw_out,
     xg, og, w, w2, g, gh, acc, ah, q, qh, pre, ga, es, er,
-    act, gp3, act3, act3t, gi, pb, rp, ps, rr, gws, ra, sbf, sb, rb, fc, rc,
+    act, gp3, act3, act3t, gi, pb, rp, ps, rr, gws, ra, sbf, sb, rb, fc, rc, zf, zs, rz, fz, rcz,
     loc_s, w2_s, ag_s, ag_r, wz_s, wz_r, wx_s, wx_r, e_s, e_r, pr_s, pr_r, rs_s, rs_r,
-    a_s, a_r, b_s, b_r, c_s, c_r,
+    a_s, a_r, b_s, b_r, c_s, c_r, d_s, d_r, f_s, f_r,
 ):
     x = lax.axis_index("dp")
     tm = lax.axis_index("tm")
@@ -443,21 +443,30 @@
         act3[t] = stacked(lambda u: act[u], t).astype(BF)
     act3t[...] = dot(eye_in[...], act3[...].reshape(1024, 192), NT).astype(BF)
 
-    first_place, size = (0, 2, 6), (2, 4, 1)
-    places = tap_places()
+    first_place, size = (0, 2), (2, 3)
+    over_x, over_z = tap_places()
 
     def x_copy(d, i):
         to = (x + d) % 4
         lo = first_place[i]
         return remote(
-            gws.at[pl.ds(7 * to + lo, size[i])], ra.at[d - 1, lo : lo + size[i]],
+            gws.at[pl.ds(5 * to + lo, size[i])], ra.at[d - 1, lo : lo + size[i]],
             a_s.at[d - 1, i], a_r.at[d - 1, i], dev(to, y, z, c),
         )
+
+    def zz_copy(d):
+        to = (z + d) % NZ
+        return remote(zs.at[to], rz.at[d - 1], d_s.at[d - 1], d_r.at[d - 1], dev(x, y, to, c))
 
     def keep(b, part):
         for e in range(3):
             for a in range(3):
-                gws[places.index((b, e, a))] = part[64 * a : 64 * a + 64, 256 * e : 256 * e + 256].astype(BF)
+                tap = part[64 * a : 64 * a + 64, 256 * e : 256 * e + 256]
+                if (b, e, a) in over_x:
+                    gws[over_x.index((b, e, a))] = tap.astype(BF)
+                else:
+                    m = over_z.index((b, e, a))
+                    zf[:, 8 * m : 8 * m + 8] = tap.reshape(8, 8, 256)
 
     def own_cells(b):
         return dot(act3t[...], g[:, :, :, 768 * b : 768 * b + 768].reshape(1024, 768), NN)
@@ -484,10 +493,12 @@
         ).astype(BF)
         hal3t = dot(eye_in[...], stack, NT).astype(BF)
         keep(2 * side, parts[side] + dot(hal3t, gh[side].reshape(256, 768), NN))
-    gws[27] = jnp.zeros((64, 256), BF)
-    for i in (1, 2):
-        for d in (2, 1, 3):
-            x_copy(d, i).start()
+    for d in (2, 1, 3):
+        x_copy(d, 1).start()
+    zf[:, 56:64] = jnp.zeros((8, 8, 256), F32)
+    zs[...] = zf[...].astype(BF)
+    for d in (4, 3, 5, 2, 6, 1, 7):
+        zz_copy(d).start()
 
     edge_wait(3)
     for t in range(8):
@@ -519,10 +530,10 @@
     pair_copy = remote(pb, rp, pr_s, pr_r, dev(x, y, z, 1 - c))
     pair_copy.start()
 
-    sbf[:, 56:64] = jnp.zeros((8, 8, 256), F32)
+    sbf[:, 40:48] = jnp.zeros((8, 8, 256), F32)
 
     def rows_of(i):
-        return slice(8 * first_place[i], 8 * first_place[i] + max(8 * size[i], 16))
+        return slice(16 * i, 16 + 32 * i)
 
     def z_copy(d, i):
         to = (z + d) % NZ
@@ -533,7 +544,7 @@
         for d in range(1, 4):
             x_copy(d, i).wait_recv()
         for j in range(first_place[i], first_place[i] + size[i]):
-            total = gws[7 * x + j].astype(F32)
+            total = gws[5 * x + j].astype(F32)
             for d in range(3):
                 total = total + ra[d, j].astype(F32)
             sbf[:, 8 * j : 8 * j + 8] = total.reshape(8, 8, 256)
@@ -564,23 +575,41 @@
     for d in (2, 1, 3):
         y_copy(d).start()
 
+    for d in range(1, NZ):
+        zz_copy(d).wait_recv()
+    total = zs[z].astype(F32)
+    for d in range(NZ - 1):
+        total = total + rz[d].astype(F32)
+    fz[...] = (total * scale).astype(BF)
+
+    def mine(to_x):
+        return jnp.logical_and(x == to_x, y == y_out)
+
+    def out_z(to_x):
+        return remote(fz, rcz.at[x], f_s.at[to_x], f_r.at[x], dev(to_x, y_out, z, c))
+
+    for to_x in range(4):
+        @pl.when(mine(to_x))
+        def _():
+            pltpu.make_async_copy(fz, rcz.at[x], f_r.at[x]).start()
+
+        @pl.when(jnp.logical_not(mine(to_x)))
+        def _():
+            out_z(to_x).start()
+
     x_sum(1)
     z_sum(0)
-    x_sum(2)
     z_sum(1)
-    z_sum(2)
 
     def out_copy(to_x):
         return remote(fc, rc.at[x], c_s.at[to_x], c_r.at[x], dev(to_x, y_out, z, c))
 
     for to_x in range(4):
-        mine = jnp.logical_and(x == to_x, y == y_out)
-
-        @pl.when(mine)
+        @pl.when(mine(to_x))
         def _():
             pltpu.make_async_copy(fc, rc.at[x], c_r.at[x]).start()
 
-        @pl.when(jnp.logical_not(mine))
+        @pl.when(jnp.logical_not(mine(to_x)))
         def _():
             out_copy(to_x).start()
 
@@ -591,13 +620,19 @@
         total = total + rr[d].astype(F32)
     gi_out[...] = total.astype(BF)
 
+    total = None
+    for part in range(4):
+        pltpu.make_async_copy(fz, rcz.at[part], f_r.at[part]).wait()
+        v = rcz[part].astype(F32)
+        total = v if total is None else total + v
+    for m, (b, e, a) in enumerate(over_z):
+        gw_out[9 * a + 3 * b + e] = total[8 * m : 8 * m + 8]
     for part in range(4):
         pltpu.make_async_copy(fc, rc.at[part], c_r.at[part]).wait()
         v = rc[part].astype(F32)
-        for j in range(7):
-            if 7 * part + j < 27:
-                b, e, a = places[7 * part + j]
-                gw_out[9 * a + 3 * b + e] = v[8 * j : 8 * j + 8]
+        for j in range(5):
+            b, e, a = over_x[5 * part + j]
+            gw_out[9 * a + 3 * b + e] = v[8 * j : 8 * j + 8]
 
     def sent(copy):
         copy.wait_send()
@@ -619,16 +654,18 @@
             edge_copy(n, side).wait_send()
     pair_copy.wait_send()
     for d in range(1, 4):
-        for i in range(3):
+        for i in range(2):
             x_copy(d, i).wait_send()
         y_copy(d).wait_send()
     for d in range(1, NZ):
-        for i in range(3):
+        zz_copy(d).wait_send()
+        for i in range(2):
             z_copy(d, i).wait_send()
     for to_x in range(4):
-        @pl.when(jnp.logical_not(jnp.logical_and(x == to_x, y == y_out)))
+        @pl.when(jnp.logical_not(mine(to_x)))
         def _():
             out_copy(to_x).wait_send()
+            out_z(to_x).wait_send()
 
 
 def on_device(latent, out_grad, w_first, w_second):
@@ -669,8 +706,13 @@
             pltpu.VMEM((2, 2, 2, 64, 512), BF),
             pltpu.VMEM((2, 2, 2, 64, 512), BF),
             pltpu.VMEM((3, 2, 64, 512), BF),
-            pltpu.VMEM((28, 64, 256), BF),
-            pltpu.VMEM((3, 7, 64, 256), BF),
+            pltpu.VMEM((20, 64, 256), BF),
+            pltpu.VMEM((3, 5, 64, 256), BF),
+            pltpu.VMEM((8, 48, 256), F32),
+            pltpu.VMEM((8, 48, 256), BF),
+            pltpu.VMEM((7, 48, 256), BF),
+            pltpu.VMEM((48, 256), BF),
+            pltpu.VMEM((4, 48, 256), BF),
             pltpu.VMEM((8, 64, 256), F32),
             pltpu.VMEM((8, 64, 256), BF),
             pltpu.VMEM((7, 64, 256), BF),
@@ -683,8 +725,10 @@
             dma((4, 2)), dma((4, 2)),
             dma, dma,
             dma((3,)), dma((3,)),
-            dma((3, 3)), dma((3, 3)),
-            dma((7, 3)), dma((7, 3)),
+            dma((3, 2)), dma((3, 2)),
+            dma((7, 2)), dma((7, 2)),
+            dma((4,)), dma((4,)),
+            dma((7,)), dma((7,)),
             dma((4,)), dma((4,)),
         ],
         compiler_params=pltpu.CompilerParams(

time: 69.1 us -> 68.6 us (level)
  no operation moved by 1% of the time
where the time goes in v6:
time: 68.6 us; the launch traced here: 68.4 us
  Pallas kernels  64.5 us (94%)
  local copies, waits for them, and re-layouts  3.2 us (5%)
    pallas_call x1, Pallas kernels, on_device(): pl.pallas_call(functools.partial(body, scale), out_shape=(jax.ShapeDtypeS...  64.5 us
    unnamed x2, local copies, waits for them, and re-layouts  3.2 us

profile of v6, /device:TPU:8, one launch (start us, length us, event | category | flops | bytes accessed | tf_op | source)
XLA Modules:
  0.0 68.4 jit_solution(1777916264326611943)
XLA Ops:
  0.6 64.5 %shard_map.77 = (bf16[2,64,512]{2,1,0:T(8,128)(2,1)}, f32[27,8,256]{2,1,0:T(8,128)}) custom-call(bf16[2,64,512]{2,1,0:T(8,128)(2,1)} %bitcast.8, bf16[2,256,256]{2,1,0:T(8,128)(2,1)} %bitcast.6, bf16[27,32,512]{2,1,0:T(8,128)(2,1)} %bitcast.5, bf16[27,512,256]{2,1,0:T(8,128)(2,1)} %w2_in.1, bf16[672,256]{1,0:T(8,128)(2,1)} %constant.4.clone.sums_in, ...), custom_call_target="tpu_custom_call" | custom-call | tf_op jit(solution)/shard_map/pallas_call | solution.py:677
  65.2 1.6 %copy.10 = bf16[1,2,4,16,512]{4,3,2,1,0:T(8,128)(2,1)} copy(bf16[1,2,4,16,512]{4,3,2,1,0:T(8,128)(2,1)} %bitcast.9) | data formatting | bytes 262144
  66.7 1.6 %copy.11 = f32[8,27,256]{2,0,1:T(8,128)} copy(f32[8,27,256]{2,0,1:T(8,128)} %bitcast.7) | data formatting | bytes 442368

commit v7 on v6

--- a/solution.py
+++ b/solution.py
@@ -224,13 +224,14 @@
     slots = (closer, 1 - closer)
     own_slot = pos % 2
 
+    for i in range(5):
+        gather(0, i).start()
+
     @pl.when(source)
     def _():
         z_sends(0, own_slot, start)
         z_sends(1, own_slot, start)
 
-    for i in range(5):
-        gather(0, i).start()
 
     @pl.when(source)
     def _():
@@ -524,11 +525,15 @@
             part = dot(rows, w[k : k + 3].reshape(192, 512), NN)
             gi[0:n] += part.reshape(n, 2, 64, 512)
 
-    for half in range(2):
+    halves = (ylo, 1 - ylo)
+
+    def pair_copy(half):
+        return remote(pb.at[half], rp.at[half], pr_s.at[half], pr_r.at[half], dev(x, y, z, 1 - c))
+
+    for half in halves:
         for f in range(2):
             pb[half, f] = gi[4 * half + 2 * (1 - c) + f].astype(BF)
-    pair_copy = remote(pb, rp, pr_s, pr_r, dev(x, y, z, 1 - c))
-    pair_copy.start()
+        pair_copy(half).start()
 
     sbf[:, 40:48] = jnp.zeros((8, 8, 256), F32)
 
@@ -563,18 +568,18 @@
         fc[part] = (total * scale).astype(BF)
 
     x_sum(0)
-    pair_copy.wait_recv()
-    for half in range(2):
-        for f in range(2):
-            ps[half, f] = (gi[4 * half + 2 * c + f] + rp[half, f].astype(F32)).astype(BF)
-
     def y_copy(d):
         to = (y + d) % 4
         return remote(ps.at[to % 2, :, to // 2], rr.at[d - 1], rs_s.at[d - 1], rs_r.at[d - 1], dev(x, to, z, c))
 
-    for d in (2, 1, 3):
-        y_copy(d).start()
-
+    for half, steps in zip(halves, ((2,), (1, 3))):
+        pair_copy(half).wait_recv()
+        for f in range(2):
+            ps[half, f] = (gi[4 * half + 2 * c + f] + rp[half, f].astype(F32)).astype(BF)
+        for d in steps:
+            y_copy(d).start()
+
+    x_sum(1)
     for d in range(1, NZ):
         zz_copy(d).wait_recv()
     total = zs[z].astype(F32)
@@ -597,7 +602,6 @@
         def _():
             out_z(to_x).start()
 
-    x_sum(1)
     z_sum(0)
     z_sum(1)
 
@@ -652,7 +656,8 @@
     for n in range(4):
         for side in range(2):
             edge_copy(n, side).wait_send()
-    pair_copy.wait_send()
+    for half in halves:
+        pair_copy(half).wait_send()
     for d in range(1, 4):
         for i in range(2):
             x_copy(d, i).wait_send()
@@ -723,7 +728,7 @@
             dma((3, 2, 4)), dma((3, 2)),
             dma((2, 6)), dma((2, 6)),
             dma((4, 2)), dma((4, 2)),
-            dma, dma,
+            dma((2,)), dma((2,)),
             dma((3,)), dma((3,)),
             dma((3, 2)), dma((3, 2)),
             dma((7, 2)), dma((7, 2)),

time: 68.6 us -> 68.1 us (level)
  Pallas kernels: 64.5 us -> 63.7 us
    pallas_call x1, Pallas kernels: 64.5 us -> 63.7 us  [on_device(): pl.pallas_call(functools.partial(body, scale), out_shape=(jax.ShapeDtypeS...]
where the time goes in v7:
time: 68.1 us; the launch traced here: 67.5 us
  Pallas kernels  63.7 us (94%)
  local copies, waits for them, and re-layouts  3.2 us (5%)
    pallas_call x1, Pallas kernels, on_device(): pl.pallas_call(functools.partial(body, scale), out_shape=(jax.ShapeDtypeS...  63.7 us
    unnamed x2, local copies, waits for them, and re-layouts  3.2 us

profile of v7, /device:TPU:8, one launch (start us, length us, event | category | flops | bytes accessed | tf_op | source)
XLA Modules:
  0.0 67.5 jit_solution(5433268550087009233)
XLA Ops:
  0.6 63.7 %shard_map.77 = (bf16[2,64,512]{2,1,0:T(8,128)(2,1)}, f32[27,8,256]{2,1,0:T(8,128)}) custom-call(bf16[2,64,512]{2,1,0:T(8,128)(2,1)} %bitcast.8, bf16[2,256,256]{2,1,0:T(8,128)(2,1)} %bitcast.6, bf16[27,32,512]{2,1,0:T(8,128)(2,1)} %bitcast.5, bf16[27,512,256]{2,1,0:T(8,128)(2,1)} %w2_in.1, bf16[672,256]{1,0:T(8,128)(2,1)} %constant.4.clone.sums_in, ...), custom_call_target="tpu_custom_call" | custom-call | tf_op jit(solution)/shard_map/pallas_call | solution.py:682
  64.3 1.6 %copy.10 = bf16[1,2,4,16,512]{4,3,2,1,0:T(8,128)(2,1)} copy(bf16[1,2,4,16,512]{4,3,2,1,0:T(8,128)(2,1)} %bitcast.9) | data formatting | bytes 262144
  65.9 1.6 %copy.11 = f32[8,27,256]{2,0,1:T(8,128)} copy(f32[8,27,256]{2,0,1:T(8,128)} %bitcast.7) | data formatting | bytes 442368
